TPU v7x, 32 devices: a whole 2x2x4 slice. The times are simulated.
32 devices in a mesh: group: 16 (over z, y, core), tp: 2 (over x).
Axes of the slice: x: 2, y: 2, z: 4, core: 2. Of those that a mesh axis runs over, the one named last changes fastest.
Arguments:
- tokens: bfloat16 [4096, 1024], P(('group', 'tp')), may hold values from -6 to 6
- variate: int32 [4096], P('group'), may hold values from 0 to 3
- time_ids: int32 [4096], P('group'), may hold values from 0 to 63
- cache_var: int32 [8192], P('group'), may hold values from 0 to 3
- cache_len: int32 [16], P('group'), may hold values from 1 to 512, as said below
- linked: int32 [16], P('group'), may hold values from 0 to 1, as said below
- cache_kv: bfloat16 [2, 8192, 1024], P(None, 'group', 'tp'), as said below
- var_bias: float32 [2, 16], P(None, 'tp'), may hold values from -2 to 2
- w_qkv: bfloat16 [3, 1024, 1024], P(None, None, 'tp'), may hold values from -0.1875 to 0.1875
- w_out: bfloat16 [1024, 1024], P('tp'), may hold values from -0.75 to 0.75
- w_gate_up: bfloat16 [2, 1024, 4096], P(None, None, 'tp'), may hold values from -0.1875 to 0.1875
- w_down: bfloat16 [4096, 1024], P('tp'), may hold values from -0.09375 to 0.09375
Outputs:
- layer_out: bfloat16 [4096, 1024], P(('group', 'tp'))
Inputs may be any that keep to these rules, and one draw needn't show every extreme that they name: Group g's cached prefix fills its first cache_len[g] slots; some group has all 512. linked[g] equals linked[g + 8]; groups 0 and 8 are linked, and some other pair is not. `cache_kv`: cached keys already rotated, and cached values.
All inputs are finite; a program needn't handle non-finite values.
Results may differ from a plain program's by a relative error of at most 0.023.
Values may be sent and summed in bfloat16 or wider, within the bound.
No kernel may reach another device: no remote copies, remote signals or barrier semaphores. Data moves between devices by JAX's collectives and lax.ppermute only.
A program may use at most 64 MiB of HBM per device.

v0:
```python
import jax
import jax.numpy as jnp
from jax import lax
from jax.sharding import PartitionSpec as P

KEY_BLOCK = 128


far_future = 1073741824
masked_score = -1e30


def from_partner(block, axis, distance):
    count = lax.axis_size(axis)
    route = []
    for low in range(count):
        high = low | 1 << distance
        if high != low and high < count:
            route += [(low, high), (high, low)]
    return lax.ppermute(block, axis, route)


def normed(row_block):
    values = row_block.astype(jnp.float32)
    return values * lax.rsqrt(jnp.mean(values * values, axis=-1, keepdims=True) + 1e-05)


def rotary(values, position, head_count):
    row_count = values.shape[0]
    shaped = values.reshape(row_count, head_count, -1)
    half_width = shaped.shape[-1] // 2
    frequency = 10000.0 ** (-jnp.arange(half_width, dtype=jnp.float32) / half_width)
    angles = position.astype(jnp.float32)[:, None] * frequency[None, :]
    cosine = jnp.cos(angles)[:, None, :]
    sine_part = jnp.sin(angles)[:, None, :]
    lower_half = shaped[..., :half_width]
    upper_half = shaped[..., half_width:]
    turned = jnp.concatenate(
        [
            lower_half * cosine - upper_half * sine_part,
            upper_half * cosine + lower_half * sine_part,
        ],
        axis=-1,
    )
    return turned.reshape(row_count, -1)


def empty_partial(head_count, row_count, width):
    return (
        jnp.full((head_count, row_count), masked_score, jnp.float32),
        jnp.zeros((head_count, row_count), jnp.float32),
        jnp.zeros((head_count, row_count, width), jnp.float32),
    )


def attend(
    running,
    queries,
    query_time,
    query_var,
    key_vals,
    key_time,
    key_var,
    bias,
    first_block,
    block_count,
):
    head_count = bias.shape[1]
    query_heads = queries.reshape(queries.shape[0], head_count, -1)

    def one_block(block_index, carried):
        row_best, total, weighted = carried
        key_start = (first_block + block_index) * KEY_BLOCK
        block_kv = lax.dynamic_slice_in_dim(key_vals, key_start, KEY_BLOCK, 1)
        block_time = lax.dynamic_slice_in_dim(key_time, key_start, KEY_BLOCK, 0)
        block_var = lax.dynamic_slice_in_dim(key_var, key_start, KEY_BLOCK, 0)
        key_heads = block_kv[0].reshape(KEY_BLOCK, head_count, -1)
        value_heads = block_kv[1].reshape(KEY_BLOCK, head_count, -1)
        scores = (
            jnp.einsum("thd,khd->htk", query_heads, key_heads, preferred_element_type=jnp.float32)
            * 0.125
        )
        same_variate = (query_var[:, None] == block_var[None, :])[None]
        scores = scores + jnp.where(same_variate, bias[0][:, None, None], bias[1][:, None, None])
        visible = (block_time[None, :] <= query_time[:, None])[None]
        scores = jnp.where(visible, scores, masked_score)
        newest = jnp.maximum(row_best, jnp.max(scores, axis=-1))
        factor = jnp.exp(row_best - newest)
        weights = jnp.exp(scores - newest[..., None])
        total = total * factor + jnp.sum(weights, axis=-1)
        weighted = weighted * factor[..., None] + jnp.einsum(
            "htk,khd->htd",
            weights.astype(jnp.bfloat16),
            value_heads,
            preferred_element_type=jnp.float32,
        )
        return (newest, total, weighted)

    return lax.fori_loop(0, block_count, one_block, running)


def shards(
    tokens,
    variate,
    time_ids,
    cache_var,
    cache_len,
    linked,
    cache_kv,
    var_bias,
    w_qkv,
    w_out,
    w_gate_up,
    w_down,
):
    head_count = var_bias.shape[1]
    cache_rows = cache_kv.shape[1]
    local_rows = tokens.shape[0]
    all_rows = lax.all_gather(tokens, "tp", axis=0, tiled=True)
    group_rows = all_rows.shape[0]
    normal_in = normed(all_rows).astype(jnp.bfloat16)
    projected = jnp.einsum("td,cde->cte", normal_in, w_qkv, preferred_element_type=jnp.float32)
    queries = rotary(projected[0], time_ids, head_count).astype(jnp.bfloat16)
    new_keys = rotary(projected[1], time_ids, head_count).astype(jnp.bfloat16)
    new_vals = projected[2].astype(jnp.bfloat16)
    head_width = new_keys.shape[1] // head_count
    own_kv = jnp.concatenate([cache_kv, jnp.stack([new_keys, new_vals])], axis=1)
    length = cache_len[0]
    linked_flag = linked[0]
    slot_ids = jnp.arange(cache_rows, dtype=jnp.int32)
    own_time = jnp.concatenate(
        [jnp.where(slot_ids < length, -1, far_future).astype(jnp.int32), time_ids]
    )
    own_var = jnp.concatenate([cache_var, variate])
    cache_blocks = cache_rows // KEY_BLOCK
    new_blocks = group_rows // KEY_BLOCK
    partner_bit = lax.axis_size("group").bit_length() - 2
    running = empty_partial(head_count, group_rows, head_width)
    running = attend(
        running, queries, time_ids, variate, own_kv, own_time, own_var, var_bias, 0, cache_blocks
    )
    running = attend(
        running,
        queries,
        time_ids,
        variate,
        own_kv,
        own_time,
        own_var,
        var_bias,
        cache_blocks,
        new_blocks,
    )
    far_kv, far_time, far_var, far_len = from_partner(
        (own_kv, own_time, own_var, cache_len), "group", partner_bit
    )
    far_time = jnp.where(linked_flag > 0, far_time, far_future).astype(jnp.int32)
    running = attend(
        running, queries, time_ids, variate, far_kv, far_time, far_var, var_bias, 0, cache_blocks
    )
    running = attend(
        running,
        queries,
        time_ids,
        variate,
        far_kv,
        far_time,
        far_var,
        var_bias,
        cache_blocks,
        new_blocks,
    )
    row_best, total, weighted = running
    attn_heads = (
        (weighted / total[..., None])
        .transpose(1, 0, 2)
        .reshape(group_rows, -1)
        .astype(jnp.bfloat16)
    )
    attended = lax.psum(
        jnp.dot(attn_heads, w_out, preferred_element_type=jnp.float32).astype(jnp.bfloat16), "tp"
    ).astype(jnp.float32)
    stream = (all_rows.astype(jnp.float32) + attended).astype(jnp.bfloat16)
    normed_mid = normed(stream).astype(jnp.bfloat16)
    gate_up = jnp.einsum("td,cdf->ctf", normed_mid, w_gate_up, preferred_element_type=jnp.float32)
    hidden = (jax.nn.silu(gate_up[0]) * gate_up[1]).astype(jnp.bfloat16)
    ffn_out = lax.psum(
        jnp.dot(hidden, w_down, preferred_element_type=jnp.float32).astype(jnp.bfloat16), "tp"
    ).astype(jnp.float32)
    row_start = lax.axis_index("tp") * local_rows
    own_stream = lax.dynamic_slice_in_dim(stream, row_start, local_rows, 0)
    own_ffn = lax.dynamic_slice_in_dim(ffn_out, row_start, local_rows, 0)
    return (own_stream.astype(jnp.float32) + own_ffn).astype(jnp.bfloat16)


def solution(mesh):
    return jax.shard_map(
        shards,
        mesh=mesh,
        in_specs=(
            P(("group", "tp"), None),
            P("group"),
            P("group"),
            P("group"),
            P("group"),
            P("group"),
            P(None, "group", "tp"),
            P(None, "tp"),
            P(None, None, "tp"),
            P("tp", None),
            P(None, None, "tp"),
            P("tp", None),
        ),
        out_specs=P(("group", "tp"), None),
        check_vma=False,
    )
```

profile of v0, /device:TPU:0, one launch (start us, length us, event | category | flops | bytes accessed | tf_op | source)
XLA Modules:
  0.0 217.6 jit_solution(6369067044309095230)
XLA Ops:
  6.6 10.3 %all_gather.3 = bf16[256,1024]{1,0:T(8,128)(2,1)S(1)} all-gather(bf16[128,1024]{1,0:T(8,128)(2,1)} %param.20), channel_id=1, replica_groups=mesh['group'=16,'tp'=2] {'tp'}, dimensions={0}, use_global_device_ids=true | all-gather | bytes 786432 | tf_op jit(solution)/shard_map/all_gather | solution.py:119
  31.0 2.3 %copy.30 = bf16[2,512,512]{1,2,0:T(8,128)(2,1)} copy(bf16[2,512,512]{2,1,0:T(8,128)(2,1)} %param.26) | data formatting | bytes 2097152 | tf_op args[6]
  33.3 2.7 %pad_maximum_fusion = bf16[2,768,512]{1,2,0:T(8,128)(2,1)} fusion(bf16[2,256,512]{1,2,0:T(8,128)(2,1)} %copy.31, bf16[2,512,512]{1,2,0:T(8,128)(2,1)} %copy.30), kind=kLoop, calls=%fused_computation.76 | loop fusion | flops 3145728 | bytes 3145728 | tf_op jit(solution)/shard_map/concatenate | solution.py:127
  36.0 2.8 %collective-permute-start.1 = (bf16[2,768,512]{1,2,0:T(8,128)(2,1)}, bf16[2,768,512]{1,2,0:T(8,128)(2,1)}, u32[]{:S(2)}, u32[]{:S(2)}) collective-permute-start(bf16[2,768,512]{1,2,0:T(8,128)(2,1)} %pad_maximum_fusion), channel_id=1, source_target_pairs={{0,16},{16,0},{2,18},{18,2},{4,20},{20,4},{6,22},{22,6},{8,24},{24... | collective-permute-start | bytes 4718600 | tf_op jit(solution)/shard_map/ppermute | solution.py:20
  42.7 2.8 %collective-permute-start = (s32[768]{0:T(1024)}, s32[768]{0:T(1024)S(1)}, u32[]{:S(2)}, u32[]{:S(2)}) collective-permute-start(s32[768]{0:T(1024)} %pad_add_fusion), channel_id=1, source_target_pairs={{0,16},{16,0},{2,18},{18,2},{4,20},{20,4},{6,22},{22,6},{8,24},{24... | collective-permute-start | bytes 9224 | tf_op jit(solution)/shard_map/ppermute | solution.py:20
  46.3 35.5 %while.72 = (s32[]{:T(128)}, f32[8,256]{1,0:T(8,128)S(1)}, f32[8,256]{1,0:T(8,128)S(1)}, f32[8,256,64]{1,2,0:T(8,128)}, s32[768]{0:T(1024)}, /*index=5*/s32[256]...) while((s32[]{:T(128)}, f32[8,256]{1,0:T(8,128)S(1)}, ...), condition=%wide.region_4.5_spmd.clone, body=%wide.region_1.4_spmd.clone.sunk | while | flops 69937160 | bytes 5510571 | solution.py:99
  48.9 2.4 %fusion.115 = (f32[8,256]{1,0:T(8,128)S(1)}, f32[8,256,128]{1,2,0:T(8,128)}) fusion(f32[8]{0:T(128)S(1)} %get-tuple-element.1273, f32[8]{0:T(128)S(1)} %get-tuple-element.1274, pred[256,128]{0,1:T(8,128)(4,1)S(1)} %get-tuple-element.1275, bf16[128,8,64]{0,2,1:T(8,128)(2,1)S(1)} %bitcast.148, bf16[256,8,64]{0,2,1:T(8,128)(2,1)} %get-tuple-element.1322, ...), kind=kOutput, calls=%fused_computation.119.clone.1 | convolution fusion | flops 34863104 | bytes 1515584 | tf_op jit(solution)/shard_map/while/body/eval_jaxpr/thd,khd->htk/dot_general | solution.py:80
  52.7 2.3 %convolution_add_fusion.11 = f32[8,256,64]{1,2,0:T(8,128)} fusion(bf16[128,8,64]{0,2,1:T(8,128)(2,1)S(1)} %bitcast.144, f32[8,256,128]{1,2,0:T(8,128)} %get-tuple-element.1279, f32[8,256,64]{1,2,0:T(8,128)} %get-tuple-element.1302, f32[8,256]{1,0:T(8,128)S(1)} %select_maximum_fusion.2, f32[8,256]{1,0:T(8,128)S(1)} %get-tuple-element.1282, ...), kind=kOutput, calls=%fused_computation.55.clone.1 | convolution fusion | flops 34471936 | bytes 2244609 | tf_op jit(solution)/shard_map/while/body/eval_jaxpr/htk,khd->htd/dot_general | solution.py:91
  57.7 2.4 %fusion.115 = (f32[8,256]{1,0:T(8,128)S(1)}, f32[8,256,128]{1,2,0:T(8,128)}) fusion(f32[8]{0:T(128)S(1)} %get-tuple-element.1273, f32[8]{0:T(128)S(1)} %get-tuple-element.1274, pred[256,128]{0,1:T(8,128)(4,1)S(1)} %get-tuple-element.1275, bf16[128,8,64]{0,2,1:T(8,128)(2,1)S(1)} %bitcast.148, bf16[256,8,64]{0,2,1:T(8,128)(2,1)} %get-tuple-element.1322, ...), kind=kOutput, calls=%fused_computation.119.clone.1 | convolution fusion | flops 34863104 | bytes 1515584 | tf_op jit(solution)/shard_map/while/body/eval_jaxpr/thd,khd->htk/dot_general | solution.py:80
  61.5 2.5 %convolution_add_fusion.11 = f32[8,256,64]{1,2,0:T(8,128)} fusion(bf16[128,8,64]{0,2,1:T(8,128)(2,1)S(1)} %bitcast.144, f32[8,256,128]{1,2,0:T(8,128)} %get-tuple-element.1279, f32[8,256,64]{1,2,0:T(8,128)} %get-tuple-element.1302, f32[8,256]{1,0:T(8,128)S(1)} %select_maximum_fusion.2, f32[8,256]{1,0:T(8,128)S(1)} %get-tuple-element.1282, ...), kind=kOutput, calls=%fused_computation.55.clone.1 | convolution fusion | flops 34471936 | bytes 2244609 | tf_op jit(solution)/shard_map/while/body/eval_jaxpr/htk,khd->htd/dot_general | solution.py:91
  66.6 2.4 %fusion.115 = (f32[8,256]{1,0:T(8,128)S(1)}, f32[8,256,128]{1,2,0:T(8,128)}) fusion(f32[8]{0:T(128)S(1)} %get-tuple-element.1273, f32[8]{0:T(128)S(1)} %get-tuple-element.1274, pred[256,128]{0,1:T(8,128)(4,1)S(1)} %get-tuple-element.1275, bf16[128,8,64]{0,2,1:T(8,128)(2,1)S(1)} %bitcast.148, bf16[256,8,64]{0,2,1:T(8,128)(2,1)} %get-tuple-element.1322, ...), kind=kOutput, calls=%fused_computation.119.clone.1 | convolution fusion | flops 34863104 | bytes 1515584 | tf_op jit(solution)/shard_map/while/body/eval_jaxpr/thd,khd->htk/dot_general | solution.py:80
  70.4 2.5 %convolution_add_fusion.11 = f32[8,256,64]{1,2,0:T(8,128)} fusion(bf16[128,8,64]{0,2,1:T(8,128)(2,1)S(1)} %bitcast.144, f32[8,256,128]{1,2,0:T(8,128)} %get-tuple-element.1279, f32[8,256,64]{1,2,0:T(8,128)} %get-tuple-element.1302, f32[8,256]{1,0:T(8,128)S(1)} %select_maximum_fusion.2, f32[8,256]{1,0:T(8,128)S(1)} %get-tuple-element.1282, ...), kind=kOutput, calls=%fused_computation.55.clone.1 | convolution fusion | flops 34471936 | bytes 2244609 | tf_op jit(solution)/shard_map/while/body/eval_jaxpr/htk,khd->htd/dot_general | solution.py:91
  75.5 2.4 %fusion.115 = (f32[8,256]{1,0:T(8,128)S(1)}, f32[8,256,128]{1,2,0:T(8,128)}) fusion(f32[8]{0:T(128)S(1)} %get-tuple-element.1273, f32[8]{0:T(128)S(1)} %get-tuple-element.1274, pred[256,128]{0,1:T(8,128)(4,1)S(1)} %get-tuple-element.1275, bf16[128,8,64]{0,2,1:T(8,128)(2,1)S(1)} %bitcast.148, bf16[256,8,64]{0,2,1:T(8,128)(2,1)} %get-tuple-element.1322, ...), kind=kOutput, calls=%fused_computation.119.clone.1 | convolution fusion | flops 34863104 | bytes 1515584 | tf_op jit(solution)/shard_map/while/body/eval_jaxpr/thd,khd->htk/dot_general | solution.py:80
  79.3 2.5 %convolution_add_fusion.11 = f32[8,256,64]{1,2,0:T(8,128)} fusion(bf16[128,8,64]{0,2,1:T(8,128)(2,1)S(1)} %bitcast.144, f32[8,256,128]{1,2,0:T(8,128)} %get-tuple-element.1279, f32[8,256,64]{1,2,0:T(8,128)} %get-tuple-element.1302, f32[8,256]{1,0:T(8,128)S(1)} %select_maximum_fusion.2, f32[8,256]{1,0:T(8,128)S(1)} %get-tuple-element.1282, ...), kind=kOutput, calls=%fused_computation.55.clone.1 | convolution fusion | flops 34471936 | bytes 2244609 | tf_op jit(solution)/shard_map/while/body/eval_jaxpr/htk,khd->htd/dot_general | solution.py:91
  81.8 12.8 %while.69 = (s32[]{:T(128)}, f32[8,256]{1,0:T(8,128)S(1)}, f32[8,256]{1,0:T(8,128)S(1)}, f32[8,256,64]{1,2,0:T(8,128)}, s32[768]{0:T(1024)}, /*index=5*/s32[256]...) while((s32[]{:T(128)}, f32[8,256]{1,0:T(8,128)S(1)}, ...), condition=%wide.region_8.9_spmd, body=%wide.region_5.8_spmd.sunk | while | flops 69799944 | bytes 5510579 | solution.py:99
  95.2 11.6 %collective-permute-done = s32[768]{0:T(1024)S(1)} collective-permute-done((s32[768]{0:T(1024)}, s32[768]{0:T(1024)S(1)}, u32[]{:S(2)}, u32[]{:S(2)}) %collective-permute-start) | collective-permute-done | bytes 3104 | tf_op jit(solution)/shard_map/ppermute | solution.py:20
  106.8 20.1 %while.70 = (s32[]{:T(128)}, f32[8,256]{1,0:T(8,128)S(1)}, f32[8,256]{1,0:T(8,128)S(1)}, f32[8,256,64]{1,2,0:T(8,128)}, s32[768]{0:T(1024)S(1)}, /*index=5*/s32[...) while((s32[]{:T(128)}, f32[8,256]{1,0:T(8,128)S(1)}, ...), condition=%wide.region_12.13_spmd, body=%wide.region_9.12_spmd.sunk | while | flops 69799944 | bytes 5510559 | solution.py:99
  126.9 10.1 %while.71 = (s32[]{:T(128)}, f32[8,256]{1,0:T(8,128)S(1)}, f32[8,256]{1,0:T(8,128)S(1)}, f32[8,256,64]{1,2,0:T(8,128)}, s32[768]{0:T(1024)S(1)}, /*index=5*/s32[...) while((s32[]{:T(128)}, f32[8,256]{1,0:T(8,128)S(1)}, ...), condition=%wide.region_16.17_spmd, body=%wide.region_13.16_spmd.sunk | while | flops 69799944 | bytes 5510579 | solution.py:99
  129.8 2.1 convolution_add_fusion.10
  138.0 2.5 %convolution_convert_fusion = bf16[256,1024]{1,0:T(8,128)(2,1)} fusion(bf16[256,512]{0,1:T(8,128)(2,1)S(1)} %bitcast.154, bf16[512,1024]{1,0:T(8,128)(2,1)} %param.29), kind=kOutput, calls=%fused_computation.83 | convolution fusion | flops 268697600 | bytes 1835008 | tf_op jit(solution)/shard_map/dot_general | solution.py:181
  140.6 29.8 %all-reduce.3.cloned.1.call-done = bf16[256,1024]{1,0:T(8,128)(2,1)} async-done(((bf16[256,1024]{1,0:T(8,128)(2,1)}), bf16[256,1024]{1,0:T(8,128)(2,1)}) %all-reduce.3.cloned.1.call-update) | async-done | bytes 524304 | tf_op jit(solution)/shard_map/psum | solution.py:180
  171.9 6.0 %convolution_bitcast_fusion = f32[2,256,2048]{2,1,0:T(8,128)S(1)} fusion(bf16[2,1024,2048]{2,1,0:T(8,128)(2,1)} %param.30, bf16[256,1024]{1,0:T(8,128)(2,1)S(1)} %get-tuple-element.892, f32[256]{0:T(256)S(1)} %add_rsqrt_fusion), kind=kOutput, calls=%fused_computation.71 | convolution fusion | flops 2148270080 | bytes 13108224 | tf_op jit(solution)/shard_map/td,cdf->ctf/dot_general | solution.py:185
  177.9 2.3 %convolution_convert_fusion.1 = bf16[256,1024]{1,0:T(8,128)(2,1)} fusion(bf16[2048,1024]{1,0:T(8,128)(2,1)S(1)} %copy-done.8, f32[2,256,2048]{2,1,0:T(8,128)S(1)} %convolution_bitcast_fusion), kind=kOutput, calls=%fused_computation.84 | convolution fusion | flops 1077149696 | bytes 8912896 | tf_op jit(solution)/shard_map/dot_general | solution.py:188
  180.3 28.7 %all-reduce.5.cloned.1.call-done = bf16[256,1024]{1,0:T(8,128)(2,1)} async-done(((bf16[256,1024]{1,0:T(8,128)(2,1)}), bf16[256,1024]{1,0:T(8,128)(2,1)}) %all-reduce.5.cloned.1.call-update) | async-done | bytes 524304 | tf_op jit(solution)/shard_map/psum | solution.py:187
  (177 shorter events, 79.0 us)
Async XLA Ops:
  6.5 10.5 %copy-start = (bf16[3,1024,512]{2,1,0:T(8,128)(2,1)S(1)}, bf16[3,1024,512]{2,1,0:T(8,128)(2,1)}, u32[]{:S(2)}) copy-start(bf16[3,1024,512]{2,1,0:T(8,128)(2,1)} %param.28) | copy-start | bytes 9437188
  6.5 163.8 %all-reduce.3.cloned.1.call-start = ((), (), s32[]{:S(2)}) async-start(), calls=%async_computation | async-start | bytes 1048576 | tf_op jit(solution)/shard_map/psum | solution.py:180
  16.8 1.2 copy-start.1
  18.1 5.9 %copy-start.4 = (s32[256]{0:T(256)S(1)}, s32[256]{0:T(256)}, u32[]{:S(2)}) copy-start(s32[256]{0:T(256)} %param.22) | copy-start | bytes 3076
  33.3 5.5 %copy-start.7 = (s32[512]{0:T(512)S(1)}, s32[512]{0:T(512)}, u32[]{:S(2)}) copy-start(s32[512]{0:T(512)} %param.23) | copy-start | bytes 6148
  33.3 6.8 %copy-start.5 = (s32[256]{0:T(256)S(1)}, s32[256]{0:T(256)}, u32[]{:S(2)}) copy-start(s32[256]{0:T(256)} %param.21) | copy-start | bytes 3076
  33.3 12.3 %copy-start.3 = (bf16[256,8,32]{0,2,1:T(8,128)(2,1)S(1)}, bf16[256,8,32]{0,2,1:T(8,128)(2,1)}, u32[]{:S(2)}) copy-start(bf16[256,8,32]{0,2,1:T(8,128)(2,1)} %get-tuple-element.928) | copy-start | bytes 393220
  33.3 13.0 %copy-start.6 = (f32[2,8]{1,0:T(2,128)S(1)}, f32[2,8]{1,0:T(2,128)}, u32[]{:S(2)}) copy-start(f32[2,8]{1,0:T(2,128)} %param.27) | copy-start | bytes 196
  36.0 70.8 %collective-permute-start.1 = (bf16[2,768,512]{1,2,0:T(8,128)(2,1)}, bf16[2,768,512]{1,2,0:T(8,128)(2,1)}, u32[]{:S(2)}, u32[]{:S(2)}) collective-permute-start(bf16[2,768,512]{1,2,0:T(8,128)(2,1)} %pad_maximum_fusion), channel_id=1, source_target_pairs={{0,16},{16,0},{2,18},{18,2},{4,20},{20,4},{6,22},{22,6},{8,24},{24... | collective-permute-start | bytes 4718600 | tf_op jit(solution)/shard_map/ppermute | solution.py:20
  41.4 65.4 %collective-permute-start.2 = (s32[768]{0:T(1024)}, s32[768]{0:T(1024)S(1)}, u32[]{:S(2)}, u32[]{:S(2)}) collective-permute-start(s32[768]{0:T(1024)} %constant_dynamic-update-slice_fusion), channel_id=1, source_target_pairs={{0,16},{16,0},{2,18},{18,2},{4,20},{20,4},{6,22},{22,6},{8,24},{24... | collective-permute-start | bytes 9224 | tf_op jit(solution)/shard_map/ppermute | solution.py:20
  42.7 64.0 %collective-permute-start = (s32[768]{0:T(1024)}, s32[768]{0:T(1024)S(1)}, u32[]{:S(2)}, u32[]{:S(2)}) collective-permute-start(s32[768]{0:T(1024)} %pad_add_fusion), channel_id=1, source_target_pairs={{0,16},{16,0},{2,18},{18,2},{4,20},{20,4},{6,22},{22,6},{8,24},{24... | collective-permute-start | bytes 9224 | tf_op jit(solution)/shard_map/ppermute | solution.py:20
  140.5 68.5 %all-reduce.5.cloned.1.call-start = ((), (), s32[]{:S(2)}) async-start(), calls=%async_computation.1 | async-start | bytes 1048576 | tf_op jit(solution)/shard_map/psum | solution.py:187
  171.8 6.1 %copy-start.2 = (bf16[256,1024]{1,0:T(8,128)(2,1)}, bf16[256,1024]{1,0:T(8,128)(2,1)S(1)}, u32[]{:S(2)}) copy-start(bf16[256,1024]{1,0:T(8,128)(2,1)S(1)} %get-tuple-element.892) | copy-start | bytes 1572868
  171.8 6.1 %copy-start.8 = (bf16[2048,1024]{1,0:T(8,128)(2,1)S(1)}, bf16[2048,1024]{1,0:T(8,128)(2,1)}, u32[]{:S(2)}) copy-start(bf16[2048,1024]{1,0:T(8,128)(2,1)} %param.31) | copy-start | bytes 12582916
Sparse Core Ops, SparseCore 0:
  140.7 29.6 all-reduce.2
  180.4 28.5 all-reduce.4
where the time goes:
time: 220 us; the launch traced here: 218 us
  waiting for transfers between devices  70.1 us (32%)
  matrix products  59.5 us (27%)
  local copies, waits for them, and re-layouts  35.6 us (16%)
  other arithmetic  20.9 us (10%)
  between operations  14.8 us (7%)
  blocking collectives  10.3 us (5%)
  starting transfers between devices  5.81 us (3%)
    psum x1, waiting for transfers between devices, shards(): lax.psum(jnp.dot(attn_heads, w_out, preferred_element_type=jnp.float32).a...  29.8 us
    psum x1, waiting for transfers between devices, shards(): lax.psum(jnp.dot(hidden, w_down, preferred_element_type=jnp.float32).asty...  28.7 us
    dot_general x12, matrix products, one_block(): jnp.einsum('htk,khd->htd', weights.astype(jnp.bfloat16), value_heads, pre...  26.9 us
    dot_general x12, matrix products, one_block(): jnp.einsum('thd,khd->htk', query_heads, key_heads, preferred_element_type...  20.7 us
    slice x12, local copies, waits for them, and re-layouts, one_block(): value_heads = block_kv[1].reshape(KEY_BLOCK, head_count, -1)  12 us
    ppermute x3, waiting for transfers between devices, from_partner(): return lax.ppermute(block, axis, route)  11.6 us
    all_gather x1, blocking collectives, shards(): all_rows = lax.all_gather(tokens, 'tp', axis=0, tiled=True)  10.3 us
    reduce_sum x12, other arithmetic, one_block(): total = total * factor + jnp.sum(weights, axis=-1)  6.8 us
  transfers between devices with their start and end apart: 5, of which 3 were waited for; matrix products, arithmetic and copies ran while one was open for 24% of the time, Pallas kernels for 0%

commit v1 on v0

v1 whole, which is shorter than its diff:
```python
import functools
import math

import jax
import jax.numpy as jnp
from jax import lax
from jax.experimental import pallas as pl
from jax.experimental.pallas import tpu as pltpu
from jax.sharding import PartitionSpec as P

LANES = 128
HEAD = 64
STAT_ROWS = 16
LOG2E = math.log2(math.e)
MASKED = -1e30
F32 = jnp.float32
BF16 = jnp.bfloat16

IN_VMEM = pl.BlockSpec(memory_space=pltpu.VMEM)
IN_SMEM = pl.BlockSpec(memory_space=pltpu.SMEM)


def call(body, outs, *operands, scalars=(), flops=0, scratch=()):
    shapes = [jax.ShapeDtypeStruct(shape, dtype) for shape, dtype in outs]
    moved = sum(x.size * x.dtype.itemsize for x in operands)
    return pl.pallas_call(
        body,
        out_shape=shapes,
        in_specs=[IN_SMEM] * len(scalars) + [IN_VMEM] * len(operands),
        out_specs=[IN_VMEM] * len(shapes),
        scratch_shapes=list(scratch),
        cost_estimate=pl.CostEstimate(flops=flops, bytes_accessed=moved, transcendentals=0),
        compiler_params=pltpu.CompilerParams(vmem_limit_bytes=32 << 20),
    )(*scalars, *operands)


def swap(block, axis, distance):
    count = lax.axis_size(axis)
    return lax.ppermute(block, axis, [(i, i ^ distance) for i in range(count)])


def normed(values):
    return (values * lax.rsqrt(jnp.mean(values * values, axis=-1, keepdims=True) + 1e-05)).astype(
        BF16
    )


def iota(shape, dim):
    return lax.broadcasted_iota(jnp.int32, shape, dim)


def dot(a, b, contract=(1, 0)):
    return lax.dot_general(
        a, b, (((contract[0],), (contract[1],)), ((), ())), preferred_element_type=F32
    )


def three_parts(value):
    high = value.astype(BF16)
    rest = value - high.astype(F32)
    middle = rest.astype(BF16)
    low = (rest - middle.astype(F32)).astype(BF16)
    return high, middle, low


def first_chunk(by_owner):
    return lax.axis_index("tp") if by_owner else 0


def row_tables(time_row, var_row):
    sub = iota((LANES, LANES), 0)
    time_hot = jnp.where((sub & (HEAD - 1)) == time_row, 1.0, 0.0).T.astype(BF16)
    var_hot = jnp.where((sub < 12) & ((sub & 3) == var_row), 1.0, 0.0).T.astype(BF16)
    half = HEAD // 2
    step = iota((half, LANES), 0).astype(F32)
    angle = time_row.astype(F32) * jnp.exp(step * (-math.log(10000.0) / half))
    cosine, sine = jnp.cos(angle), jnp.sin(angle)
    cosine = jnp.concatenate([cosine] * 4, axis=0).T
    sine = jnp.concatenate([-sine, sine, -sine, sine], axis=0).T
    return time_hot, var_hot, cosine, sine


def own_tables(
    by_owner, heads, length, bias, time, var, cache_var, time_hot, var_hot, cosine, sine, mask, key_hot, shift
):
    first = first_chunk(by_owner)
    sub = iota((LANES, LANES), 0)
    cache_chunks = cache_var.shape[0]
    for chunk in range(cache_chunks):
        slot = sub + chunk * LANES
        mask[chunk] = jnp.where(slot >= length[0], MASKED, 0.0).astype(BF16)
        row = cache_var[chunk : chunk + 1, :]
        key_hot[chunk] = jnp.where((sub < 12) & ((sub & 3) == row), 1.0, 0.0).T.astype(BF16)
    for chunk in range(2):
        place = chunk if not by_owner else (first if chunk == 0 else 1 - first)
        time_row = time[pl.ds(place, 1), :]
        tables = row_tables(time_row, var[pl.ds(place, 1), :])
        time_hot[chunk], var_hot[chunk], cosine[chunk], sine[chunk] = tables
        key_hot[cache_chunks + chunk] = tables[1]
        later = jnp.where(time_row > (sub & (HEAD - 1)), MASKED, 0.0)
        mask[cache_chunks + chunk] = later.T.astype(BF16)
    lane = iota((1, LANES), 1)
    for head in range(heads):
        gain = jnp.full((1, LANES), (bias[0, head] - bias[1, head]) * LOG2E, F32)
        high, middle, low = (part.astype(F32) for part in three_parts(gain))
        row = jnp.where(lane < 4, high, jnp.where(lane < 8, middle, jnp.where(lane < 12, low, 0.0)))
        shift[head : head + 1, :] = row


def far_tables(by_owner, time, var, time_hot, var_hot, cosine, sine):
    first = first_chunk(by_owner)
    for chunk in range(2):
        place = chunk if not by_owner else (first if chunk == 0 else 1 - first)
        tables = row_tables(time[pl.ds(place, 1), :], var[pl.ds(place, 1), :])
        time_hot[chunk], var_hot[chunk], cosine[chunk], sine[chunk] = tables


def turned(values, cosine, sine):
    lane = iota(values.shape, 1)
    quarter = HEAD // 2
    other = jnp.where(
        (lane & (HEAD - 1)) < quarter,
        pltpu.roll(values, LANES - quarter, 1),
        pltpu.roll(values, quarter, 1),
    )
    return values * cosine + other * sine


def blocks(width):
    return [slice(start, start + LANES) for start in range(0, width, LANES)]


def project(first, second, weight, cosine, sine, queries, keys, values, rows):
    for chunk, block in enumerate((first, second)):
        rows[chunk * LANES : (chunk + 1) * LANES, :] = normed(block[...].astype(F32))
    for part, target in enumerate((queries, keys, values)):
        product = dot(rows[...], weight[part])
        for chunk in range(2):
            for cols in blocks(product.shape[1]):
                piece = product[chunk * LANES : (chunk + 1) * LANES, cols]
                if part < 2:
                    piece = turned(piece, cosine[chunk], sine[chunk])
                if part == 0:
                    piece = piece * (0.125 * LOG2E)
                target[chunk, :, cols] = piece.astype(BF16)


def attend_pair(pair, query, time_hot, var_hot, shift, keys, values, mask, key_hot):
    lane = iota((LANES, LANES), 1)
    key_lane = iota(keys.shape, 1)
    weighted, best = [], []
    for side in range(2):
        head = 2 * pair + side
        in_head = (lane < HEAD) if side == 0 else (lane >= HEAD)
        key_in_head = (key_lane < HEAD) if side == 0 else (key_lane >= HEAD)
        gain = shift[head : head + 1, :].astype(BF16)
        left = jnp.concatenate([jnp.where(in_head, query, time_hot), var_hot * gain], axis=1)
        right = jnp.concatenate([jnp.where(key_in_head, keys, mask), key_hot], axis=1)
        scores = dot(left, right, (1, 1))
        top = jnp.max(scores, axis=1, keepdims=True)
        weights = jnp.exp2(scores - top).astype(BF16)
        weighted.append(dot(weights, jnp.where(key_in_head, values, jnp.ones_like(values))))
        best.append(top)
    low = lane < HEAD
    total = pltpu.roll(jnp.where(low, weighted[1], weighted[0]), HEAD, 1)
    outputs = jnp.where(low, weighted[0], weighted[1]) / total
    return outputs, jnp.where(low, best[0], best[1]) + jnp.log2(total)


def key_block(index, cols, cache, fresh):
    return jnp.concatenate([cache[index, :, cols], fresh[0, :, cols], fresh[1, :, cols]], axis=0)


def attend_own(queries, time_hot, var_hot, shift, keys, values, cache, mask, key_hot, outputs, logs):
    all_mask = mask[...].reshape(-1, LANES)
    all_hot = key_hot[...].reshape(-1, LANES)
    for pair, cols in enumerate(blocks(queries.shape[2])):
        pair_keys = key_block(0, cols, cache, keys)
        pair_values = key_block(1, cols, cache, values)
        for chunk in range(2):
            out, log = attend_pair(
                pair, queries[chunk, :, cols], time_hot[chunk], var_hot[chunk], shift[...],
                pair_keys, pair_values, all_mask, all_hot,
            )
            outputs[chunk, :, cols] = out
            logs[chunk, :, cols] = log


def stat_place(part, width):
    count = width // LANES
    return part % count, (part // count) * (width // HEAD)


def attend_far(
    chunk, tokens, weight, cosine, sine, time_hot, var_hot, shift, keys, values, cache, mask, key_hot, message
):
    width = message.shape[1]
    product = dot(normed(tokens[...].astype(F32)), weight[0])
    all_mask = mask[...].reshape(-1, LANES)
    all_hot = key_hot[...].reshape(-1, LANES)
    stats = [jnp.zeros((STAT_ROWS, LANES), F32) for _ in blocks(width)]
    for pair, cols in enumerate(blocks(width)):
        query = turned(product[:, cols], cosine[chunk], sine[chunk]) * (0.125 * LOG2E)
        out, log = attend_pair(
            pair, query.astype(BF16), time_hot[chunk], var_hot[chunk], shift[...],
            key_block(0, cols, cache, keys), key_block(1, cols, cache, values), all_mask, all_hot,
        )
        message[:LANES, cols] = out.astype(BF16)
        row, lane = iota((STAT_ROWS, LANES), 0), iota((STAT_ROWS, LANES), 1)
        for part, piece in enumerate(three_parts(log)):
            block, offset = stat_place(part, width)
            pick = (row - offset - 2 * pair) * HEAD == lane
            stats[block] += dot(jnp.where(pick, 1.0, 0.0).astype(BF16), piece, (1, 1))
    for block, cols in zip(stats, blocks(width), strict=True):
        message[LANES:, cols] = block.astype(BF16)


def join(chunk, linked, own, own_log, message, weight, kept, sent):
    width = message.shape[1]
    pieces = []
    row = iota((STAT_ROWS, LANES), 0)
    lane = iota((STAT_ROWS, LANES), 1)
    for pair, cols in enumerate(blocks(width)):
        far_log = jnp.zeros((LANES, LANES), F32)
        for part in range(3):
            block, offset = stat_place(part, width)
            stat = message[LANES:, block * LANES : (block + 1) * LANES]
            pick = row - offset - 2 * pair == lane // HEAD
            far_log += dot(stat, jnp.where(pick, 1.0, 0.0).astype(BF16), (0, 0))
        far_log = jnp.where(linked[0] > 0, far_log, MASKED)
        share = 1.0 / (1.0 + jnp.exp2(far_log - own_log[chunk, :, cols]))
        far = message[:LANES, cols].astype(F32)
        pieces.append((far + (own[chunk, :, cols] - far) * share).astype(BF16))
    product = dot(jnp.concatenate(pieces, axis=1), weight[...])
    kept[...] = product
    sent[...] = product.astype(BF16)


def feed(final, tokens, kept, received, gate_up, down, out):
    stream = (tokens[...].astype(F32) + kept[...] + received[...].astype(F32)).astype(BF16)
    stream = stream.astype(F32)
    rows = normed(stream)
    gate = dot(rows, gate_up[0])
    hidden = (gate / (1.0 + jnp.exp(-gate)) * dot(rows, gate_up[1])).astype(BF16)
    product = dot(hidden, down[...])
    out[...] = stream + product if final else product.astype(BF16)


def shards(
    tokens,
    variate,
    time_ids,
    cache_var,
    cache_len,
    linked,
    cache_kv,
    var_bias,
    w_qkv,
    w_out,
    w_gate_up,
    w_down,
):
    heads = var_bias.shape[1]
    width = cache_kv.shape[2]
    model = tokens.shape[1]
    cache_rows = cache_kv.shape[1]
    ways = lax.axis_size("tp")
    partner = lax.axis_size("group") // 2
    paired = ways == 2
    chunk = (LANES, LANES)
    key_chunks = cache_rows // LANES + 2

    far_tokens = swap(tokens, "group", partner)
    time, var = time_ids.reshape(2, LANES), variate.reshape(2, LANES)
    far_time, far_var = (swap(ids, "group", partner) for ids in (time, var))
    if paired:
        own_rows = (tokens, swap(tokens, "tp", 1))
    else:
        gathered = lax.all_gather(tokens, "tp", axis=0, tiled=True)
        own_rows = (gathered[:LANES], gathered[LANES:])

    time_hot, var_hot, cosine, sine, mask, key_hot, shift = call(
        functools.partial(own_tables, paired, heads),
        [((2, *chunk), BF16), ((2, *chunk), BF16), ((2, *chunk), F32), ((2, *chunk), F32)]
        + [((key_chunks, *chunk), BF16), ((key_chunks, *chunk), BF16), ((heads, LANES), F32)],
        time, var, cache_var.reshape(-1, LANES), scalars=(cache_len, var_bias),
    )
    far_time_hot, far_var_hot, far_cosine, far_sine = call(
        functools.partial(far_tables, paired),
        [((2, *chunk), BF16), ((2, *chunk), BF16), ((2, *chunk), F32), ((2, *chunk), F32)],
        far_time, far_var,
    )
    queries, keys, values = call(
        project, [((2, LANES, width), BF16)] * 3,
        *own_rows, w_qkv, cosine, sine,
        flops=6 * 256 * model * width, scratch=[pltpu.VMEM((2 * LANES, model), BF16)],
    )
    if paired:
        far_rows = (far_tokens, swap(far_tokens, "tp", 1))
    else:
        gathered = lax.all_gather(far_tokens, "tp", axis=0, tiled=True)
        far_rows = (gathered[:LANES], gathered[LANES:])

    key_side = (shift, keys, values, cache_kv, mask, key_hot)
    own, own_log = call(
        attend_own, [((2, LANES, width), F32)] * 2,
        queries, time_hot, var_hot, *key_side, flops=4 * 256 * 768 * width * 4,
    )
    returned = []
    for index in range(2):
        (message,) = call(
            functools.partial(attend_far, index), [((LANES + STAT_ROWS, width), BF16)],
            far_rows[index], w_qkv, far_cosine, far_sine, far_time_hot, far_var_hot, *key_side,
            flops=4 * 128 * 768 * width * 4,
        )
        returned.append(swap(message, "group", partner))
    kept, sent = [], []
    for index in range(2):
        products = call(
            functools.partial(join, index), [((LANES, model), F32), ((LANES, model), BF16)],
            own, own_log, returned[index], w_out, scalars=(linked,), flops=2 * 128 * width * model,
        )
        kept.append(products[0])
        sent.append(products[1])

    def fed(index, final, part, received):
        (out,) = call(
            functools.partial(feed, final), [((LANES, model), F32 if final else BF16)],
            own_rows[index], part, received, w_gate_up, w_down,
            flops=6 * 128 * model * w_down.shape[0],
        )
        return out

    if paired:
        from_first = swap(sent[0], "tp", 1)
        from_second = swap(sent[1], "tp", 1)
        other = swap(fed(1, False, kept[1], from_first), "tp", 1)
        mine = fed(0, True, kept[0], from_second)
        return (mine + other.astype(F32)).astype(BF16)
    attended = [lax.psum(part, "tp") for part in sent]
    nothing = jnp.zeros((LANES, model), F32)
    parts = jnp.concatenate([fed(i, False, nothing, attended[i]) for i in range(2)])
    summed = lax.psum(parts, "tp")
    local = tokens.shape[0]
    start = lax.axis_index("tp") * local
    attended = lax.dynamic_slice_in_dim(jnp.concatenate(attended), start, local, 0)
    stream = (tokens.astype(F32) + attended.astype(F32)).astype(BF16).astype(F32)
    own_ffn = lax.dynamic_slice_in_dim(summed, start, local, 0).astype(F32)
    return (stream + own_ffn).astype(BF16)


def solution(mesh):
    return jax.shard_map(
        shards,
        mesh=mesh,
        in_specs=(
            P(("group", "tp"), None),
            P("group"),
            P("group"),
            P("group"),
            P("group"),
            P("group"),
            P(None, "group", "tp"),
            P(None, "tp"),
            P(None, None, "tp"),
            P("tp", None),
            P(None, None, "tp"),
            P("tp", None),
        ),
        out_specs=P(("group", "tp"), None),
        check_vma=False,
    )
```

time: 220 us -> 63.6 us (0.29)
  matrix products: 59.5 us -> 0 us
  waiting for transfers between devices: 70.1 us -> 16.7 us
  local copies, waits for them, and re-layouts: 35.6 us -> 7.61 us
  Pallas kernels: 0 us -> 22.9 us
  other arithmetic: 20.9 us -> 0.76 us
  between operations: 14.8 us -> 1.44 us
  blocking collectives: 10.3 us -> 0 us
  starting transfers between devices: 5.81 us -> 13.8 us
    dot_general x28 -> x0, matrix products: 59.5 us -> none  [the longest x12 26.9 us: one_block(): jnp.einsum('htk,khd->htd', weights.astype(jnp.bfloat16), value_heads, pre...]
    psum x2 -> x0, waiting for transfers between devices: 58.5 us -> none  [the longest x1 29.8 us: shards(): lax.psum(jnp.dot(attn_heads, w_out, preferred_element_type=jnp.float32).a...]
    pallas_call x0 -> x10, Pallas kernels: none -> 22.9 us  [call(): pl.pallas_call(body, out_shape=shapes, in_specs=[IN_SMEM] * len(scalars)...]
    slice x16 -> x0, local copies, waits for them, and re-layouts: 17.9 us -> none  [the longest x12 12 us: one_block(): value_heads = block_kv[1].reshape(KEY_BLOCK, head_count, -1)]
    all_gather x1 -> x0, blocking collectives: 10.3 us -> none  [shards(): all_rows = lax.all_gather(tokens, 'tp', axis=0, tiled=True)]
    dynamic_slice x24 -> x0, local copies, waits for them, and re-layouts: 9.89 us -> none  [the longest x12 4.97 us: one_block(): block_var = lax.dynamic_slice_in_dim(key_var, key_start, KEY_BLOCK, 0)]
    reduce_sum x14 -> x0, other arithmetic: 8.45 us -> none  [the longest x12 6.8 us: one_block(): total = total * factor + jnp.sum(weights, axis=-1)]
    ppermute x3 -> x10, starting transfers between devices: 5.76 us -> 13.8 us  [swap(): return lax.ppermute(block, axis, [(i, i ^ distance) for i in range(count)])]
  transfers between devices with their start and end apart: 5 -> 10, of which waited for: 3 -> 5; matrix products, arithmetic and copies ran while one was open for 24% -> 0% of each run, Pallas kernels for 0% -> 36%
where the time goes in v1:
time: 63.6 us; the launch traced here: 63.2 us
  Pallas kernels  22.9 us (36%)
  waiting for transfers between devices  16.7 us (26%)
  starting transfers between devices  13.8 us (22%)
  local copies, waits for them, and re-layouts  7.61 us (12%)
  between operations  1.44 us (2%)
  other arithmetic  0.76 us (1%)
    pallas_call x10, Pallas kernels, call(): pl.pallas_call(body, out_shape=shapes, in_specs=[IN_SMEM] * len(scalars)...  22.9 us
    ppermute x10, waiting for transfers between devices, swap(): return lax.ppermute(block, axis, [(i, i ^ distance) for i in range(count)])  16.7 us
    ppermute x10, starting transfers between devices, swap(): return lax.ppermute(block, axis, [(i, i ^ distance) for i in range(count)])  13.8 us
    unnamed x26, local copies, waits for them, and re-layouts  7.61 us
  transfers between devices with their start and end apart: 10, of which 5 were waited for; matrix products, arithmetic and copies ran while one was open for 0% of the time, Pallas kernels for 36%

profile of v1, /device:TPU:0, one launch (start us, length us, event | category | flops | bytes accessed | tf_op | source)
XLA Modules:
  0.0 63.2 jit_solution(8088643136171528189)
XLA Ops:
  0.0 4.0 %collective-permute-start.1 = (bf16[128,1024]{1,0:T(8,128)(2,1)}, bf16[128,1024]{1,0:T(8,128)(2,1)S(1)}, u32[]{:S(2)}, u32[]{:S(2)}) collective-permute-start(bf16[128,1024]{1,0:T(8,128)(2,1)} %tokens.1), channel_id=1, source_target_pairs={{0,16},{2,18},{4,20},{6,22},{8,24},{10,26},{12,28},{14,30},{16,0},... | collective-permute-start | bytes 786440 | tf_op jit(solution)/shard_map/ppermute | solution.py:39
  4.0 1.5 %collective-permute-start = (bf16[128,1024]{1,0:T(8,128)(2,1)}, bf16[128,1024]{1,0:T(8,128)(2,1)S(1)}, u32[]{:S(2)}, u32[]{:S(2)}) collective-permute-start(bf16[128,1024]{1,0:T(8,128)(2,1)} %tokens.1), channel_id=1, source_target_pairs={{0,1},{1,0},{2,3},{3,2},{4,5},{5,4},{6,7},{7,6},{8,9},{9,8},{10,11... | collective-permute-start | bytes 786440 | tf_op jit(solution)/shard_map/ppermute | solution.py:39
  5.9 2.6 %collective-permute-start.2 = (s32[2,128]{1,0:T(2,128)}, s32[2,128]{1,0:T(2,128)S(1)}, u32[]{:S(2)}, u32[]{:S(2)}) collective-permute-start(s32[2,128]{1,0:T(2,128)} %bitcast.8), channel_id=1, source_target_pairs={{0,16},{2,18},{4,20},{6,22},{8,24},{10,26},{12,28},{14,30},{16,0},... | collective-permute-start | bytes 3080 | tf_op jit(solution)/shard_map/ppermute | solution.py:39
  10.4 0.7 %copy-done.8 = f32[2,8]{1,0:T(2,128)S(1)} copy-done((f32[2,8]{1,0:T(2,128)S(1)}, f32[2,8]{1,0:T(2,128)}, u32[]{:S(2)}) %copy-start.8) | copy-done | bytes 88
  12.5 0.9 %shard_map.118 = (bf16[2,128,128]{2,1,0:T(8,128)(2,1)S(1)}, bf16[2,128,128]{2,1,0:T(8,128)(2,1)S(1)}, f32[2,128,128]{2,1,0:T(8,128)S(1)}, f32[2,128,128]{2,1,0:T...) custom-call(s32[1]{0:T(128)S(6)} %copy.13.length, ...), custom_call_target="tpu_custom_call" | custom-call | bytes 4096 | tf_op jit(solution)/shard_map/pallas_call | solution.py:26
  13.4 2.9 %collective-permute-done.3.var = s32[2,128]{1,0:T(2,128)S(1)} collective-permute-done((s32[2,128]{1,0:T(2,128)}, s32[2,128]{1,0:T(2,128)S(1)}, u32[]{:S(2)}, u32[]{:S(2)}) %collective-permute-start.3) | collective-permute-done | bytes 1056 | tf_op jit(solution)/shard_map/ppermute | solution.py:39
  16.6 1.6 %collective-permute-start.5 = (bf16[128,1024]{1,0:T(8,128)(2,1)S(1)}, bf16[128,1024]{1,0:T(8,128)(2,1)S(1)}, u32[]{:S(2)}, u32[]{:S(2)}) collective-permute-start(bf16[128,1024]{1,0:T(8,128)(2,1)S(1)} %collective-permute-done.1.tokens), channel_id=1, source_target_pairs={{0,1},{1,0},{2,3},{3,2},{4,5},{5,4},{6,7},{7,6},{8,9},{9,8},{10,11... | collective-permute-start | bytes 786440 | tf_op jit(solution)/shard_map/ppermute | solution.py:39
  18.2 1.9 %copy-done = bf16[3,1024,512]{2,1,0:T(8,128)(2,1)S(1)} copy-done((bf16[3,1024,512]{2,1,0:T(8,128)(2,1)S(1)}, bf16[3,1024,512]{2,1,0:T(8,128)(2,1)}, u32[]{:S(2)}) %copy-start) | copy-done | bytes 3145752
  20.1 0.9 %copy-done.5 = bf16[128,1024]{1,0:T(8,128)(2,1)S(1)} copy-done((bf16[128,1024]{1,0:T(8,128)(2,1)S(1)}, bf16[128,1024]{1,0:T(8,128)(2,1)}, u32[]{:S(2)}) %copy-start.5) | copy-done | bytes 262168
  21.0 1.1 %shard_map.119 = (bf16[2,128,512]{2,1,0:T(8,128)(2,1)S(1)}, bf16[2,128,512]{2,1,0:T(8,128)(2,1)S(1)}, bf16[2,128,512]{2,1,0:T(8,128)(2,1)S(1)}) custom-call(bf16[128,1024]{1,0:T(8,128)(2,1)S(1)} %copy-done.5, bf16[128,1024]{1,0:T(8,128)(2,1)S(1)} %collective-permute-done.second.tokens, bf16[3,1024,512]{2,1,0:T(8,128)(2,1)S(1)} %copy-done, ...), custom_call_target="tpu_custom_call" | custom-call | flops 805306368 | bytes 3932160 | tf_op jit(solution)/shard_map/pallas_call | solution.py:26
  22.1 0.8 %copy-done.1 = bf16[3,1024,512]{2,1,0:T(8,128)(2,1)S(1)} copy-done((bf16[3,1024,512]{2,1,0:T(8,128)(2,1)S(1)}, bf16[3,1024,512]{2,1,0:T(8,128)(2,1)}, u32[]{:S(2)}) %copy-start.1) | copy-done | bytes 3145752
  22.9 1.2 %copy-done.3 = bf16[2,512,512]{2,1,0:T(8,128)(2,1)S(1)} copy-done((bf16[2,512,512]{2,1,0:T(8,128)(2,1)S(1)}, bf16[2,512,512]{2,1,0:T(8,128)(2,1)}, u32[]{:S(2)}) %copy-start.3) | copy-done | bytes 1048600
  24.1 4.4 %shard_map.122 = bf16[144,512]{1,0:T(8,128)(2,1)S(1)} custom-call(bf16[128,1024]{1,0:T(8,128)(2,1)S(1)} %collective-permute-done.1.tokens, bf16[3,1024,512]{2,1,0:T(8,128)(2,1)S(1)} %copy-done.1, f32[2,128,128]{2,1,0:T(8,128)S(1)} %get-tuple-element.37.cosine, f32[2,128,128]{2,1,0:T(8,128)S(1)} %get-tuple-element.38.sine, ...), custom_call_target="tpu_custom_call" | custom-call | flops 805306368 | bytes 5771264 | tf_op jit(solution)/shard_map/pallas_call | solution.py:26
  28.6 6.8 %shard_map.120 = (f32[2,128,512]{2,1,0:T(8,128)S(1)}, f32[2,128,512]{2,1,0:T(8,128)S(1)}) custom-call(bf16[2,128,512]{2,1,0:T(8,128)(2,1)S(1)} %get-tuple-element.27.queries, bf16[2,128,128]{2,1,0:T(8,128)(2,1)S(1)} %get-tuple-element.28.time_hot, bf16[2,128,128]{2,1,0:T(8,128)(2,1)S(1)} %get-tuple-element.29.var_hot, f32[8,128]{1,0:T(8,128)S(1)} %get-tuple-element.30.shift, ...), custom_call_target="tpu_custom_call" | custom-call | flops 1610612736 | bytes 2363392 | tf_op jit(solution)/shard_map/pallas_call | solution.py:26
  35.4 2.0 %collective-permute-done.4.message = bf16[144,512]{1,0:T(8,128)(2,1)S(1)} collective-permute-done((bf16[144,512]{1,0:T(8,128)(2,1)S(1)}, bf16[144,512]{1,0:T(8,128)(2,1)S(1)}, u32[]{:S(2)}, u32[]{:S(2)}) %collective-permute-start.4) | collective-permute-done | bytes 147488 | tf_op jit(solution)/shard_map/ppermute | solution.py:39
  38.5 4.5 %shard_map.124 = bf16[144,512]{1,0:T(8,128)(2,1)S(1)} custom-call(bf16[128,1024]{1,0:T(8,128)(2,1)S(1)} %collective-permute-done.5.tokens, bf16[3,1024,512]{2,1,0:T(8,128)(2,1)S(1)} %copy-done.1, f32[2,128,128]{2,1,0:T(8,128)S(1)} %get-tuple-element.37.cosine, f32[2,128,128]{2,1,0:T(8,128)S(1)} %get-tuple-element.38.sine, ...), custom_call_target="tpu_custom_call" | custom-call | flops 805306368 | bytes 5771264 | tf_op jit(solution)/shard_map/pallas_call | solution.py:26
  43.0 0.9 %collective-permute-start.6 = (bf16[144,512]{1,0:T(8,128)(2,1)S(1)}, bf16[144,512]{1,0:T(8,128)(2,1)S(1)}, u32[]{:S(2)}, u32[]{:S(2)}) collective-permute-start(bf16[144,512]{1,0:T(8,128)(2,1)S(1)} %shard_map.124), channel_id=1, source_target_pairs={{0,16},{2,18},{4,20},{6,22},{8,24},{10,26},{12,28},{14,30},{16,0},... | collective-permute-start | bytes 442376 | tf_op jit(solution)/shard_map/ppermute | solution.py:39
  43.9 8.0 %collective-permute-done.6.message = bf16[144,512]{1,0:T(8,128)(2,1)S(1)} collective-permute-done((bf16[144,512]{1,0:T(8,128)(2,1)S(1)}, bf16[144,512]{1,0:T(8,128)(2,1)S(1)}, u32[]{:S(2)}, u32[]{:S(2)}) %collective-permute-start.6) | collective-permute-done | bytes 147488 | tf_op jit(solution)/shard_map/ppermute | solution.py:39
  52.5 1.6 %collective-permute-start.7 = (bf16[128,1024]{1,0:T(8,128)(2,1)S(1)}, bf16[128,1024]{1,0:T(8,128)(2,1)S(1)}, u32[]{:S(2)}, u32[]{:S(2)}) collective-permute-start(bf16[128,1024]{1,0:T(8,128)(2,1)S(1)} %get-tuple-element.42), channel_id=1, source_target_pairs={{0,1},{1,0},{2,3},{3,2},{4,5},{5,4},{6,7},{7,6},{8,9},{9,8},{10,11... | collective-permute-start | bytes 786440 | tf_op jit(solution)/shard_map/ppermute | solution.py:39
  54.1 2.0 %shard_map.127 = bf16[128,1024]{1,0:T(8,128)(2,1)S(1)} custom-call(bf16[128,1024]{1,0:T(8,128)(2,1)S(1)} %collective-permute-done.second.tokens, f32[128,1024]{1,0:T(8,128)S(1)} %get-tuple-element.43.kept, bf16[128,1024]{1,0:T(8,128)(2,1)S(1)} %collective-permute-done.8.received, bf16[2,1024,2048]{2,1,0:T(8,128)(2,1)S(1)} %bitcast.4, ...), custom_call_target="tpu_custom_call" | custom-call | flops 1610612736 | bytes 13631488 | tf_op jit(solution)/shard_map/pallas_call | solution.py:26
  56.6 2.3 %collective-permute-done.7.received = bf16[128,1024]{1,0:T(8,128)(2,1)S(1)} collective-permute-done((bf16[128,1024]{1,0:T(8,128)(2,1)S(1)}, bf16[128,1024]{1,0:T(8,128)(2,1)S(1)}, u32[]{:S(2)}, u32[]{:S(2)}) %collective-permute-start.7) | collective-permute-done | bytes 262176 | tf_op jit(solution)/shard_map/ppermute | solution.py:39
  58.9 2.0 %shard_map.126 = f32[128,1024]{1,0:T(8,128)S(1)} custom-call(bf16[128,1024]{1,0:T(8,128)(2,1)S(1)} %copy-done.6, f32[128,1024]{1,0:T(8,128)S(1)} %get-tuple-element.41.kept, bf16[128,1024]{1,0:T(8,128)(2,1)S(1)} %collective-permute-done.7.received, bf16[2,1024,2048]{2,1,0:T(8,128)(2,1)S(1)} %bitcast.4, bf16[2048,1024]{1,0:T(8,128)(2,1)S(1)} %copy-done.2), custom_call_target="tpu_custom_call" | custom-call | flops 1610612736 | bytes 13631488 | tf_op jit(solution)/shard_map/pallas_call | solution.py:26
  60.9 1.6 %collective-permute-done.9 = bf16[128,1024]{1,0:T(8,128)(2,1)S(1)} collective-permute-done((bf16[128,1024]{1,0:T(8,128)(2,1)S(1)}, bf16[128,1024]{1,0:T(8,128)(2,1)S(1)}, u32[]{:S(2)}, u32[]{:S(2)}) %collective-permute-start.9) | collective-permute-done | bytes 262176 | tf_op jit(solution)/shard_map/ppermute | solution.py:39
  62.5 0.8 %add_convert_fusion = bf16[128,1024]{1,0:T(8,128)(2,1)} fusion(f32[128,1024]{1,0:T(8,128)S(1)} %shard_map.126, bf16[128,1024]{1,0:T(8,128)(2,1)S(1)} %collective-permute-done.9), kind=kLoop, calls=%fused_computation | loop fusion | flops 393216 | bytes 1048576 | tf_op jit(solution)/shard_map/convert_element_type | solution.py:339
  (34 shorter events, 5.1 us)
Async XLA Ops:
  0.0 16.6 %collective-permute-start.1 = (bf16[128,1024]{1,0:T(8,128)(2,1)}, bf16[128,1024]{1,0:T(8,128)(2,1)S(1)}, u32[]{:S(2)}, u32[]{:S(2)}) collective-permute-start(bf16[128,1024]{1,0:T(8,128)(2,1)} %tokens.1), channel_id=1, source_target_pairs={{0,16},{2,18},{4,20},{6,22},{8,24},{10,26},{12,28},{14,30},{16,0},... | collective-permute-start | bytes 786440 | tf_op jit(solution)/shard_map/ppermute | solution.py:39
  4.0 14.1 %collective-permute-start = (bf16[128,1024]{1,0:T(8,128)(2,1)}, bf16[128,1024]{1,0:T(8,128)(2,1)S(1)}, u32[]{:S(2)}, u32[]{:S(2)}) collective-permute-start(bf16[128,1024]{1,0:T(8,128)(2,1)} %tokens.1), channel_id=1, source_target_pairs={{0,1},{1,0},{2,3},{3,2},{4,5},{5,4},{6,7},{7,6},{8,9},{9,8},{10,11... | collective-permute-start | bytes 786440 | tf_op jit(solution)/shard_map/ppermute | solution.py:39
  5.5 10.8 %collective-permute-start.3 = (s32[2,128]{1,0:T(2,128)}, s32[2,128]{1,0:T(2,128)S(1)}, u32[]{:S(2)}, u32[]{:S(2)}) collective-permute-start(s32[2,128]{1,0:T(2,128)} %bitcast.6), channel_id=1, source_target_pairs={{0,16},{2,18},{4,20},{6,22},{8,24},{10,26},{12,28},{14,30},{16,0},... | collective-permute-start | bytes 3080 | tf_op jit(solution)/shard_map/ppermute | solution.py:39
  5.9 10.4 %collective-permute-start.2 = (s32[2,128]{1,0:T(2,128)}, s32[2,128]{1,0:T(2,128)S(1)}, u32[]{:S(2)}, u32[]{:S(2)}) collective-permute-start(s32[2,128]{1,0:T(2,128)} %bitcast.8), channel_id=1, source_target_pairs={{0,16},{2,18},{4,20},{6,22},{8,24},{10,26},{12,28},{14,30},{16,0},... | collective-permute-start | bytes 3080 | tf_op jit(solution)/shard_map/ppermute | solution.py:39
  9.8 0.7 %copy-start.7 = (s32[512]{0:T(512)S(1)}, s32[512]{0:T(512)}, u32[]{:S(2)}) copy-start(s32[512]{0:T(512)} %param.15) | copy-start | bytes 6148
  10.4 0.7 %copy-start.8 = (f32[2,8]{1,0:T(2,128)S(1)}, f32[2,8]{1,0:T(2,128)}, u32[]{:S(2)}) copy-start(f32[2,8]{1,0:T(2,128)} %bias.1) | copy-start | bytes 196
  11.1 0.7 %copy-start.9 = (s32[256]{0:T(256)S(1)}, s32[256]{0:T(256)}, u32[]{:S(2)}) copy-start(s32[256]{0:T(256)} %param.13) | copy-start | bytes 3076
  11.8 0.7 %copy-start.10 = (s32[256]{0:T(256)S(1)}, s32[256]{0:T(256)}, u32[]{:S(2)}) copy-start(s32[256]{0:T(256)} %param.14) | copy-start | bytes 3076
  16.6 21.9 %collective-permute-start.5 = (bf16[128,1024]{1,0:T(8,128)(2,1)S(1)}, bf16[128,1024]{1,0:T(8,128)(2,1)S(1)}, u32[]{:S(2)}, u32[]{:S(2)}) collective-permute-start(bf16[128,1024]{1,0:T(8,128)(2,1)S(1)} %collective-permute-done.1.tokens), channel_id=1, source_target_pairs={{0,1},{1,0},{2,3},{3,2},{4,5},{5,4},{6,7},{7,6},{8,9},{9,8},{10,11... | collective-permute-start | bytes 786440 | tf_op jit(solution)/shard_map/ppermute | solution.py:39
  18.2 1.9 %copy-start = (bf16[3,1024,512]{2,1,0:T(8,128)(2,1)S(1)}, bf16[3,1024,512]{2,1,0:T(8,128)(2,1)}, u32[]{:S(2)}) copy-start(bf16[3,1024,512]{2,1,0:T(8,128)(2,1)} %weight.8) | copy-start | bytes 9437188
  20.1 0.9 %copy-start.5 = (bf16[128,1024]{1,0:T(8,128)(2,1)S(1)}, bf16[128,1024]{1,0:T(8,128)(2,1)}, u32[]{:S(2)}) copy-start(bf16[128,1024]{1,0:T(8,128)(2,1)} %tokens.1) | copy-start | bytes 786436
  21.0 1.9 %copy-start.1 = (bf16[3,1024,512]{2,1,0:T(8,128)(2,1)S(1)}, bf16[3,1024,512]{2,1,0:T(8,128)(2,1)}, u32[]{:S(2)}) copy-start(bf16[3,1024,512]{2,1,0:T(8,128)(2,1)} %weight.8) | copy-start | bytes 9437188
  22.9 1.2 %copy-start.3 = (bf16[2,512,512]{2,1,0:T(8,128)(2,1)S(1)}, bf16[2,512,512]{2,1,0:T(8,128)(2,1)}, u32[]{:S(2)}) copy-start(bf16[2,512,512]{2,1,0:T(8,128)(2,1)} %cache.5) | copy-start | bytes 3145732
  28.5 8.8 %copy-start.4 = (bf16[512,1024]{1,0:T(8,128)(2,1)S(1)}, bf16[512,1024]{1,0:T(8,128)(2,1)}, u32[]{:S(2)}) copy-start(bf16[512,1024]{1,0:T(8,128)(2,1)} %weight.9) | copy-start | bytes 3145732
  28.5 8.8 %collective-permute-start.4 = (bf16[144,512]{1,0:T(8,128)(2,1)S(1)}, bf16[144,512]{1,0:T(8,128)(2,1)S(1)}, u32[]{:S(2)}, u32[]{:S(2)}) collective-permute-start(bf16[144,512]{1,0:T(8,128)(2,1)S(1)} %shard_map.122), channel_id=1, source_target_pairs={{0,16},{2,18},{4,20},{6,22},{8,24},{10,26},{12,28},{14,30},{16,0},... | collective-permute-start | bytes 442376 | tf_op jit(solution)/shard_map/ppermute | solution.py:39
  28.6 25.5 %slice-start = ((s8[8388608]{0:T(1024)(128)(4,1)}), s8[4194304]{0:T(1024)(128)(4,1)S(1)}, s32[]{:S(2)}) async-start(s8[8388608]{0:T(1024)(128)(4,1)} %bitcast.3), calls=%async_computation | async-start | bytes 8388608
  37.3 16.7 %slice-start.1 = ((s8[8388608]{0:T(1024)(128)(4,1)}), s8[4194304]{0:T(1024)(128)(4,1)S(1)}, s32[]{:S(2)}) async-start(s8[8388608]{0:T(1024)(128)(4,1)} %bitcast.3), calls=%async_computation.1 | async-start | bytes 8388608
  37.9 16.2 %copy-start.2 = (bf16[2048,1024]{1,0:T(8,128)(2,1)S(1)}, bf16[2048,1024]{1,0:T(8,128)(2,1)}, u32[]{:S(2)}) copy-start(bf16[2048,1024]{1,0:T(8,128)(2,1)} %down.3) | copy-start | bytes 12582916
  37.9 16.1 %collective-permute-start.8 = (bf16[128,1024]{1,0:T(8,128)(2,1)S(1)}, bf16[128,1024]{1,0:T(8,128)(2,1)S(1)}, u32[]{:S(2)}, u32[]{:S(2)}) collective-permute-start(bf16[128,1024]{1,0:T(8,128)(2,1)S(1)} %get-tuple-element.44), channel_id=1, source_target_pairs={{0,1},{1,0},{2,3},{3,2},{4,5},{5,4},{6,7},{7,6},{8,9},{9,8},{10,11... | collective-permute-start | bytes 786440 | tf_op jit(solution)/shard_map/ppermute | solution.py:39
  43.0 8.9 %collective-permute-start.6 = (bf16[144,512]{1,0:T(8,128)(2,1)S(1)}, bf16[144,512]{1,0:T(8,128)(2,1)S(1)}, u32[]{:S(2)}, u32[]{:S(2)}) collective-permute-start(bf16[144,512]{1,0:T(8,128)(2,1)S(1)} %shard_map.124), channel_id=1, source_target_pairs={{0,16},{2,18},{4,20},{6,22},{8,24},{10,26},{12,28},{14,30},{16,0},... | collective-permute-start | bytes 442376 | tf_op jit(solution)/shard_map/ppermute | solution.py:39
  52.5 6.4 %collective-permute-start.7 = (bf16[128,1024]{1,0:T(8,128)(2,1)S(1)}, bf16[128,1024]{1,0:T(8,128)(2,1)S(1)}, u32[]{:S(2)}, u32[]{:S(2)}) collective-permute-start(bf16[128,1024]{1,0:T(8,128)(2,1)S(1)} %get-tuple-element.42), channel_id=1, source_target_pairs={{0,1},{1,0},{2,3},{3,2},{4,5},{5,4},{6,7},{7,6},{8,9},{9,8},{10,11... | collective-permute-start | bytes 786440 | tf_op jit(solution)/shard_map/ppermute | solution.py:39
  54.1 4.9 %copy-start.6 = (bf16[128,1024]{1,0:T(8,128)(2,1)S(1)}, bf16[128,1024]{1,0:T(8,128)(2,1)}, u32[]{:S(2)}) copy-start(bf16[128,1024]{1,0:T(8,128)(2,1)} %tokens.1) | copy-start | bytes 786436
  56.0 6.4 %collective-permute-start.9 = (bf16[128,1024]{1,0:T(8,128)(2,1)S(1)}, bf16[128,1024]{1,0:T(8,128)(2,1)S(1)}, u32[]{:S(2)}, u32[]{:S(2)}) collective-permute-start(bf16[128,1024]{1,0:T(8,128)(2,1)S(1)} %shard_map.127), channel_id=1, source_target_pairs={{0,1},{1,0},{2,3},{3,2},{4,5},{5,4},{6,7},{7,6},{8,9},{9,8},{10,11... | collective-permute-start | bytes 786440 | tf_op jit(solution)/shard_map/ppermute | solution.py:39

commit v2 on v1

v2 whole, which is shorter than its diff:
```python
import functools
import math

import jax
import jax.numpy as jnp
from jax import lax
from jax.experimental import pallas as pl
from jax.experimental.pallas import tpu as pltpu
from jax.sharding import PartitionSpec as P

LANES = 128
HEAD = 64
HALF = HEAD // 2
LOG_ROWS = 8
STAT_ROWS = 32
LOG2E = math.log2(math.e)
MASKED = -1e30
F32 = jnp.float32
BF16 = jnp.bfloat16

IN_VMEM = pl.BlockSpec(memory_space=pltpu.VMEM)
IN_SMEM = pl.BlockSpec(memory_space=pltpu.SMEM)


def call(body, outs, *operands, scalars=(), flops=0, scratch=()):
    shapes = [jax.ShapeDtypeStruct(shape, dtype) for shape, dtype in outs]
    moved = sum(x.size * x.dtype.itemsize for x in operands)
    return pl.pallas_call(
        body,
        out_shape=shapes,
        in_specs=[IN_SMEM] * len(scalars) + [IN_VMEM] * len(operands),
        out_specs=[IN_VMEM] * len(shapes),
        scratch_shapes=list(scratch),
        cost_estimate=pl.CostEstimate(flops=flops, bytes_accessed=moved, transcendentals=0),
        compiler_params=pltpu.CompilerParams(vmem_limit_bytes=16 << 20),
    )(*scalars, *operands)


def swap(block, axis, distance):
    count = lax.axis_size(axis)
    return lax.ppermute(block, axis, [(i, i ^ distance) for i in range(count)])


def normed(values):
    return (values * lax.rsqrt(jnp.mean(values * values, axis=-1, keepdims=True) + 1e-05)).astype(
        BF16
    )


def iota(shape, dim):
    return lax.broadcasted_iota(jnp.int32, shape, dim)


def dot(a, b):
    return jnp.dot(a, b, preferred_element_type=F32)


def three_parts(value):
    high = value.astype(BF16).astype(F32)
    middle = (value - high).astype(BF16).astype(F32)
    low = (value - high - middle).astype(BF16).astype(F32)
    return high, middle, low


def blocks(width):
    return [slice(start, start + LANES) for start in range(0, width, LANES)]


def place_of(chunk, by_owner):
    if not by_owner:
        return chunk
    return lax.axis_index("tp") if chunk == 0 else 1 - lax.axis_index("tp")


def ids_of(small, chunk, by_owner):
    ids = small[pl.ds(place_of(chunk, by_owner), 1), :].astype(jnp.int32)
    return ids & (HEAD - 1), ids >> 6


def query_tables(time_row, var_row):
    time_hot = jnp.where(iota((HEAD, LANES), 0) == time_row, 1.0, 0.0).astype(BF16)
    sub = iota((16, LANES), 0)
    var_hot = jnp.where((sub < 12) & ((sub & 3) == var_row), 1.0, 0.0).astype(BF16)
    angle = time_row.astype(F32) * jnp.exp(
        iota((HALF, LANES), 0).astype(F32) * (-math.log(10000.0) / HALF)
    )
    return time_hot, var_hot, jnp.cos(angle), jnp.sin(angle)


def key_table(hidden, var_row):
    sub = iota((LANES - HEAD, LANES), 0)
    same = jnp.where((sub < 12) & ((sub & 3) == var_row), 1.0, 0.0)
    return jnp.concatenate([jnp.where(hidden, MASKED, 0.0), same], axis=0).T.astype(BF16)


def tables(
    by_owner, heads, length, small, time_hot, var_hot, cosine, sine, key_cosine, key_sine, key_hot, gains
):
    cache_chunks = key_hot.shape[0] - 2
    for chunk in range(cache_chunks):
        slot = iota((HEAD, LANES), 1) + chunk * LANES
        cache_var = small[chunk + 2 : chunk + 3, :].astype(jnp.int32)
        key_hot[chunk] = key_table(slot >= length[0], cache_var)
    for chunk in range(2):
        time_row, var_row = ids_of(small, chunk, by_owner)
        time_hot[chunk], var_hot[chunk], cos, sin = query_tables(time_row, var_row)
        cosine[chunk], sine[chunk] = cos, sin
        key_cosine[chunk] = jnp.concatenate([cos] * 4, axis=0).T
        key_sine[chunk] = jnp.concatenate([-sin, sin, -sin, sin], axis=0).T
        key_hot[cache_chunks + chunk] = key_table(time_row > iota((HEAD, LANES), 0), var_row)
    sub = iota((16, LANES), 0)
    bias = small[cache_chunks + 2 : cache_chunks + 3, :] * LOG2E
    for head in range(heads):
        gain = bias[:, head : head + 1] - bias[:, heads + head : heads + head + 1]
        high, middle, low = three_parts(jnp.broadcast_to(gain, (16, LANES)))
        gains[head] = jnp.where(sub < 4, high, jnp.where(sub < 8, middle, low)).astype(BF16)


def arrange(cache, cache_values):
    for rows in blocks(cache.shape[1]):
        for cols in blocks(cache.shape[2]):
            cache_values[cols, rows] = cache[1, rows, cols].T


def turn_queries(piece, cosine, sine):
    turned = []
    for start in range(0, LANES, HEAD):
        x, y = piece[start : start + HALF, :], piece[start + HALF : start + HEAD, :]
        turned += [x * cosine - y * sine, y * cosine + x * sine]
    return (jnp.concatenate(turned, axis=0) * (0.125 * LOG2E)).astype(BF16)


def turn_keys(piece, cosine, sine):
    first = (iota(piece.shape, 1) & (HEAD - 1)) < HALF
    other = jnp.where(first, pltpu.roll(piece, LANES - HALF, 1), pltpu.roll(piece, HALF, 1))
    return (piece * cosine + other * sine).astype(BF16)


def project(
    first, second, weight, cosine, sine, key_cosine, key_sine, queries, keys, values, rows
):
    for chunk, block in enumerate((first, second)):
        rows[chunk * LANES : (chunk + 1) * LANES, :] = normed(block[...].astype(F32))
    for part in (1, 0, 2):
        product = dot(rows[...], weight[part])
        for chunk in range(2):
            for cols in blocks(product.shape[1]):
                piece = product[chunk * LANES : (chunk + 1) * LANES, cols]
                if part == 0:
                    queries[chunk, cols, :] = turn_queries(piece.T, cosine[chunk], sine[chunk])
                elif part == 1:
                    keys[chunk, :, cols] = turn_keys(piece, key_cosine[chunk], key_sine[chunk])
                else:
                    values[chunk, cols, :] = piece.T.astype(BF16)


def attend(queries, time_hot, var_hot, gains, keys, values, cache, cache_values, key_hot, emit):
    hot = key_hot[...].reshape(-1, LANES)
    ones = jnp.ones((16, hot.shape[0]), BF16)
    blank = jnp.zeros((HEAD, LANES), BF16)
    rest = jnp.zeros((LANES - HEAD - 16, LANES), BF16)
    chunks, width = len(queries), cache_values.shape[0]
    units = [(pair, chunk) for pair in range(width // LANES) for chunk in range(chunks)]
    left, right = [], []
    for cols in blocks(width):
        block = [cache[0, :, cols], keys[0, :, cols], keys[1, :, cols]]
        left.append(jnp.concatenate([jnp.concatenate(block, axis=0), hot], axis=1))
        block = [cache_values[cols, :], values[0, cols, :], values[1, cols, :]]
        right.append(jnp.concatenate([jnp.concatenate(block, axis=1), ones], axis=0))

    def features(pair, chunk):
        sides = []
        for side in range(2):
            head = 2 * pair + side
            query = queries[chunk][head * HEAD : (head + 1) * HEAD, :]
            both = [query, blank] if side == 0 else [blank, query]
            sides.append(
                jnp.concatenate(
                    both + [time_hot[chunk], var_hot[chunk] * gains[head], rest], axis=0
                )
            )
        return jnp.concatenate(sides, axis=1)

    scores, weights = {}, {}
    for step in range(len(units) + 2):
        if step < len(units):
            pair, chunk = units[step]
            scores[step] = dot(left[pair], features(pair, chunk))
        if 0 <= step - 1 < len(units):
            score = scores.pop(step - 1)
            top = jnp.max(score, axis=0, keepdims=True)
            weights[step - 1] = jnp.exp2(score - top).astype(BF16), top
        if 0 <= step - 2 < len(units):
            pair, chunk = units[step - 2]
            weight, top = weights.pop(step - 2)
            product = dot(right[pair], weight)
            for side in range(2):
                head, lanes = 2 * pair + side, slice(side * LANES, (side + 1) * LANES)
                total = product[LANES : LANES + 1, lanes]
                out = product[side * HEAD : (side + 1) * HEAD, lanes] * (1.0 / total)
                emit(chunk, head, out, top[:, lanes] + jnp.log2(total))


def attend_own(
    queries, time_hot, var_hot, gains, keys, values, cache, cache_values, key_hot, outputs, logs
):
    def emit(chunk, head, out, log):
        outputs[chunk, head * HEAD : (head + 1) * HEAD, :] = out
        logs[chunk, head : head + 1, :] = log

    rows = [queries.at[chunk] for chunk in range(2)]
    attend(
        rows, time_hot, var_hot, gains, keys, values, cache, cache_values, key_hot, emit
    )


def attend_far(
    chunk, by_owner, small, tokens, weight, gains, keys, values, cache, cache_values, key_hot, message, queries, logs
):
    width = cache_values.shape[0]
    time_hot, var_hot, cosine, sine = query_tables(*ids_of(small, chunk, by_owner))
    product = dot(normed(tokens[...].astype(F32)), weight[0])
    for cols in blocks(width):
        queries[cols, :] = turn_queries(product[:, cols].T, cosine, sine)
    logs[...] = jnp.zeros_like(logs)

    def emit(_, head, out, log):
        message[head * HEAD : (head + 1) * HEAD, :] = out.astype(BF16)
        logs[head : head + 1, :] = log

    attend(
        [queries], [time_hot], [var_hot], gains, keys, values, cache, cache_values, key_hot, emit
    )
    parts = list(three_parts(logs[...])) + [jnp.zeros((LOG_ROWS, LANES), F32)]
    message[width:, :] = jnp.concatenate(parts, axis=0).astype(BF16)


def join(chunk, linked, own, own_log, message, weight, kept, sent):
    width = weight.shape[0]
    stats = message[width:, :].astype(F32)
    far_log = stats[:8, :] + stats[8:16, :] + stats[16:24, :]
    far_log = jnp.where(linked[0] > 0, far_log, MASKED)
    share = 1.0 / (1.0 + jnp.exp2(far_log - own_log[chunk]))
    pieces = []
    for cols in blocks(width):
        joined = []
        for start in range(cols.start, cols.stop, HEAD):
            rows, head = slice(start, start + HEAD), start // HEAD
            far = message[rows, :].astype(F32)
            joined.append(far + (own[chunk, rows, :] - far) * share[head : head + 1, :])
        pieces.append(jnp.concatenate(joined, axis=0).T.astype(BF16))
    product = dot(jnp.concatenate(pieces, axis=1), weight[...])
    kept[...] = product
    sent[...] = product.astype(BF16)


def feed(final, tokens, kept, received, gate_up, down, out):
    stream = (tokens[...].astype(F32) + kept[...] + received[...].astype(F32)).astype(BF16)
    stream = stream.astype(F32)
    rows = normed(stream)
    gate = dot(rows, gate_up[0])
    hidden = (gate / (1.0 + jnp.exp(-gate)) * dot(rows, gate_up[1])).astype(BF16)
    product = dot(hidden, down[...])
    out[...] = stream + product if final else product.astype(BF16)


def shards(
    tokens,
    variate,
    time_ids,
    cache_var,
    cache_len,
    linked,
    cache_kv,
    var_bias,
    w_qkv,
    w_out,
    w_gate_up,
    w_down,
):
    heads = var_bias.shape[1]
    width = cache_kv.shape[2]
    model = tokens.shape[1]
    cache_rows = cache_kv.shape[1]
    ways = lax.axis_size("tp")
    partner = lax.axis_size("group") // 2
    paired = ways == 2
    key_chunks = cache_rows // LANES + 2

    far_tokens = swap(tokens, "group", partner)
    ids, held = lax.optimization_barrier(((time_ids + HEAD * variate).astype(F32), tokens))
    if paired:
        other_tokens = swap(held, "tp", 1)
    small = jnp.concatenate(
        [
            ids,
            cache_var.astype(F32),
            jnp.pad(var_bias.reshape(-1), (0, LANES - 2 * heads)),
        ]
    ).reshape(-1, LANES)
    far_small = swap(small, "group", partner)
    time_hot, var_hot, cosine, sine, key_cosine, key_sine, key_hot, gains = call(
        functools.partial(tables, paired, heads),
        [((2, HEAD, LANES), BF16), ((2, 16, LANES), BF16), ((2, HALF, LANES), F32), ((2, HALF, LANES), F32)]
        + [((2, LANES, LANES), F32)] * 2
        + [((key_chunks, LANES, LANES), BF16), ((heads, 16, LANES), BF16)],
        small, scalars=(cache_len,), flops=6_000_000_000,
    )
    (cache_values,) = call(arrange, [((width, cache_rows), BF16)], cache_kv)

    def all_rows(mine, other):
        if paired:
            return mine, other
        gathered = lax.all_gather(mine, "tp", axis=0, tiled=True)
        return gathered[:LANES], gathered[LANES:]

    own_rows = all_rows(tokens, other_tokens if paired else None)
    queries, keys, values = call(
        project,
        [((2, width, LANES), BF16), ((2, LANES, width), BF16), ((2, width, LANES), BF16)],
        *own_rows, w_qkv, cosine, sine, key_cosine, key_sine,
        flops=6 * 256 * model * width, scratch=[pltpu.VMEM((2 * LANES, model), BF16)],
    )
    key_side = (gains, keys, values, cache_kv, cache_values, key_hot)
    own, own_log = call(
        attend_own, [((2, width, LANES), F32), ((2, LOG_ROWS, LANES), F32)],
        queries, time_hot, var_hot, *key_side, flops=8 * 256 * 768 * width,
    )
    far_tokens, far_small, own = lax.optimization_barrier((far_tokens, far_small, own))
    far_rows = all_rows(far_tokens, swap(far_tokens, "tp", 1) if paired else None)
    messages = []
    for index in range(2):
        (message,) = call(
            functools.partial(attend_far, index, paired), [((width + STAT_ROWS, LANES), BF16)],
            far_small, far_rows[index], w_qkv, *key_side, flops=8 * 128 * 768 * width,
            scratch=[pltpu.VMEM((width, LANES), BF16), pltpu.VMEM((LOG_ROWS, LANES), F32)],
        )
        messages.append(message)
    returned = [swap(message, "group", partner) for message in messages]
    returned[0], _ = lax.optimization_barrier((returned[0], messages[1]))
    kept, sent = [], []
    for index in range(2):
        products = call(
            functools.partial(join, index), [((LANES, model), F32), ((LANES, model), BF16)],
            own, own_log, returned[index], w_out, scalars=(linked,), flops=2 * 128 * width * model,
        )
        kept.append(products[0])
        sent.append(products[1])

    def fed(index, final, part, received):
        (out,) = call(
            functools.partial(feed, final), [((LANES, model), F32 if final else BF16)],
            own_rows[index], part, received, w_gate_up, w_down,
            flops=6 * 128 * model * w_down.shape[0],
        )
        return out

    if paired:
        from_first = swap(sent[0], "tp", 1)
        from_second = swap(sent[1], "tp", 1)
        other = swap(fed(1, False, kept[1], from_first), "tp", 1)
        mine = fed(0, True, kept[0], from_second)
        return (mine + other.astype(F32)).astype(BF16)
    attended = [lax.psum(part, "tp") for part in sent]
    nothing = jnp.zeros((LANES, model), F32)
    parts = jnp.concatenate([fed(i, False, nothing, attended[i]) for i in range(2)])
    summed = lax.psum(parts, "tp")
    local = tokens.shape[0]
    start = lax.axis_index("tp") * local
    attended = lax.dynamic_slice_in_dim(jnp.concatenate(attended), start, local, 0)
    stream = (tokens.astype(F32) + attended.astype(F32)).astype(BF16).astype(F32)
    own_ffn = lax.dynamic_slice_in_dim(summed, start, local, 0).astype(F32)
    return (stream + own_ffn).astype(BF16)


def solution(mesh):
    return jax.shard_map(
        shards,
        mesh=mesh,
        in_specs=(
            P(("group", "tp"), None),
            P("group"),
            P("group"),
            P("group"),
            P("group"),
            P("group"),
            P(None, "group", "tp"),
            P(None, "tp"),
            P(None, None, "tp"),
            P("tp", None),
            P(None, None, "tp"),
            P("tp", None),
        ),
        out_specs=P(("group", "tp"), None),
        check_vma=False,
    )
```

time: 63.6 us -> 48.7 us (0.77)
  Pallas kernels: 22.9 us -> 12.3 us
  local copies, waits for them, and re-layouts: 7.61 us -> 1.66 us
  other arithmetic: 0.76 us -> 2.15 us
    pallas_call x10, Pallas kernels: 22.9 us -> 12.3 us  [call(): pl.pallas_call(body, out_shape=shapes, in_specs=[IN_SMEM] * len(scalars)...]
    unnamed x26 -> x14, local copies, waits for them, and re-layouts: 7.61 us -> 0.9 us
    convert_element_type x0 -> x2, other arithmetic: none -> 1.38 us  [the longest x1 0.7 us: shards(): (time_ids + HEAD * variate).astype(F32)]
    reshape x0 -> x1, local copies, waits for them, and re-layouts: none -> 0.76 us  [shards(): var_bias.reshape(-1)]
    ppermute x10 -> x9, waiting for transfers between devices: 16.7 us -> 17 us  [swap(): return lax.ppermute(block, axis, [(i, i ^ distance) for i in range(count)])]
    ppermute x10 -> x9, starting transfers between devices: 13.8 us -> 13.9 us  [swap(): return lax.ppermute(block, axis, [(i, i ^ distance) for i in range(count)])]
  transfers between devices with their start and end apart: 10 -> 9, of which waited for: 5 -> 6; matrix products, arithmetic and copies ran while one was open for 0% -> 4% of each run, Pallas kernels for 36% -> 25%
where the time goes in v2:
time: 48.7 us; the launch traced here: 48.5 us
  waiting for transfers between devices  17 us (35%)
  starting transfers between devices  13.9 us (29%)
  Pallas kernels  12.3 us (25%)
  other arithmetic  2.15 us (4%)
  local copies, waits for them, and re-layouts  1.66 us (3%)
  between operations  1.47 us (3%)
    ppermute x9, waiting for transfers between devices, swap(): return lax.ppermute(block, axis, [(i, i ^ distance) for i in range(count)])  17 us
    ppermute x9, starting transfers between devices, swap(): return lax.ppermute(block, axis, [(i, i ^ distance) for i in range(count)])  13.9 us
    pallas_call x10, Pallas kernels, call(): pl.pallas_call(body, out_shape=shapes, in_specs=[IN_SMEM] * len(scalars)...  12.3 us
  transfers between devices with their start and end apart: 9, of which 6 were waited for; matrix products, arithmetic and copies ran while one was open for 4% of the time, Pallas kernels for 25%

profile of v2, /device:TPU:0, one launch (start us, length us, event | category | flops | bytes accessed | tf_op | source)
XLA Modules:
  0.0 48.5 jit_solution(17084295940602205085)
XLA Ops:
  0.0 4.0 %collective-permute-start = (bf16[128,1024]{1,0:T(8,128)(2,1)}, bf16[128,1024]{1,0:T(8,128)(2,1)S(1)}, u32[]{:S(2)}, u32[]{:S(2)}) collective-permute-start(bf16[128,1024]{1,0:T(8,128)(2,1)} %tokens.1), channel_id=1, source_target_pairs={{0,16},{2,18},{4,20},{6,22},{8,24},{10,26},{12,28},{14,30},{16,0},... | collective-permute-start | bytes 786440 | tf_op jit(solution)/shard_map/ppermute | solution.py:41
  4.0 0.8 %reshape.6 = f32[16]{0:T(128)S(1)} reshape(f32[2,8]{1,0:T(2,128)} %param.19) | data formatting | bytes 128 | tf_op jit(solution)/shard_map/reshape | solution.py:298
  4.8 0.7 %add_convert_fusion.1 = f32[256]{0:T(256)S(1)} fusion(s32[256]{0:T(256)} %param.14, s32[256]{0:T(256)} %param.13), kind=kLoop, calls=%fused_computation.4 | loop fusion | flops 768 | bytes 3072 | tf_op jit(solution)/shard_map/convert_element_type | solution.py:291
  5.5 0.7 %convert_element_type.15 = f32[512]{0:T(512)S(1)} convert(s32[512]{0:T(512)} %param.15) | non-fusion elementwise | flops 512 | bytes 4096 | tf_op jit(solution)/shard_map/convert_element_type | solution.py:297
  6.3 1.8 %collective-permute-start.2 = (bf16[128,1024]{1,0:T(8,128)(2,1)}, bf16[128,1024]{1,0:T(8,128)(2,1)S(1)}, u32[]{:S(2)}, u32[]{:S(2)}) collective-permute-start(bf16[128,1024]{1,0:T(8,128)(2,1)} %tokens.1), channel_id=1, source_target_pairs={{0,1},{1,0},{2,3},{3,2},{4,5},{5,4},{6,7},{7,6},{8,9},{9,8},{10,11... | collective-permute-start | bytes 786440 | tf_op jit(solution)/shard_map/ppermute | solution.py:41
  9.1 0.9 %copy-done.2 = bf16[2,512,512]{2,1,0:T(8,128)(2,1)S(1)} copy-done((bf16[2,512,512]{2,1,0:T(8,128)(2,1)S(1)}, bf16[2,512,512]{2,1,0:T(8,128)(2,1)}, u32[]{:S(2)}) %copy-start.2) | copy-done | bytes 1048600
  10.1 4.2 %collective-permute-done.2.second.tokens = bf16[128,1024]{1,0:T(8,128)(2,1)S(1)} collective-permute-done((bf16[128,1024]{1,0:T(8,128)(2,1)}, bf16[128,1024]{1,0:T(8,128)(2,1)S(1)}, u32[]{:S(2)}, u32[]{:S(2)}) %collective-permute-start.2) | collective-permute-done | bytes 262176 | tf_op jit(solution)/shard_map/ppermute | solution.py:41
  14.3 1.2 %shard_map.119 = (bf16[2,512,128]{2,1,0:T(8,128)(2,1)S(1)}, bf16[2,128,512]{2,1,0:T(8,128)(2,1)S(1)}, bf16[2,512,128]{2,1,0:T(8,128)(2,1)S(1)}) custom-call(bf16[128,1024]{1,0:T(8,128)(2,1)S(1)} %copy-done.4, bf16[128,1024]{1,0:T(8,128)(2,1)S(1)} %collective-permute-done.2.second.tokens, bf16[3,1024,512]{2,1,0:T(8,128)(2,1)S(1)} %copy-done, ...), custom_call_target="tpu_custom_call" | custom-call | flops 805306368 | bytes 3997696 | tf_op jit(solution)/shard_map/pallas_call | solution.py:28
  15.5 2.2 %shard_map.121 = (f32[2,512,128]{2,1,0:T(8,128)S(1)}, f32[2,8,128]{2,1,0:T(8,128)S(1)}) custom-call(bf16[2,512,128]{2,1,0:T(8,128)(2,1)S(1)} %get-tuple-element.34.queries, bf16[2,64,128]{2,1,0:T(8,128)(2,1)S(1)} %get-tuple-element.35.time_hot, bf16[2,16,128]{2,1,0:T(8,128)(2,1)S(1)} %get-tuple-element.36.var_hot, ...), custom_call_target="tpu_custom_call" | custom-call | flops 805306368 | bytes 2629632 | tf_op jit(solution)/shard_map/pallas_call | solution.py:28
  17.7 1.6 %collective-permute-start.4 = (bf16[128,1024]{1,0:T(8,128)(2,1)S(1)}, bf16[128,1024]{1,0:T(8,128)(2,1)S(1)}, u32[]{:S(2)}, u32[]{:S(2)}) collective-permute-start(bf16[128,1024]{1,0:T(8,128)(2,1)S(1)} %collective-permute-done.tokens), channel_id=1, source_target_pairs={{0,1},{1,0},{2,3},{3,2},{4,5},{5,4},{6,7},{7,6},{8,9},{9,8},{10,11... | collective-permute-start | bytes 786440 | tf_op jit(solution)/shard_map/ppermute | solution.py:41
  19.3 1.9 %shard_map.122 = bf16[544,128]{1,0:T(8,128)(2,1)S(1)} custom-call(f32[7,128]{1,0:T(8,128)S(1)} %collective-permute-done.1.small, bf16[128,1024]{1,0:T(8,128)(2,1)S(1)} %collective-permute-done.tokens, bf16[3,1024,512]{2,1,0:T(8,128)(2,1)S(1)} %copy-done, bf16[8,16,128]{2,1,0:T(8,128)(2,1)S(1)} %get-tuple-element.37.gains, ...), custom_call_target="tpu_custom_call" | custom-call | flops 402653184 | bytes 5737984 | tf_op jit(solution)/shard_map/pallas_call | solution.py:28
  21.2 2.6 %collective-permute-start.3 = (bf16[544,128]{1,0:T(8,128)(2,1)S(1)}, bf16[544,128]{1,0:T(8,128)(2,1)S(1)}, u32[]{:S(2)}, u32[]{:S(2)}) collective-permute-start(bf16[544,128]{1,0:T(8,128)(2,1)S(1)} %shard_map.122), channel_id=1, source_target_pairs={{0,16},{2,18},{4,20},{6,22},{8,24},{10,26},{12,28},{14,30},{16,0},... | collective-permute-start | bytes 417800 | tf_op jit(solution)/shard_map/ppermute | solution.py:41
  24.7 1.9 %shard_map.123 = bf16[544,128]{1,0:T(8,128)(2,1)S(1)} custom-call(f32[7,128]{1,0:T(8,128)S(1)} %collective-permute-done.1.small, bf16[128,1024]{1,0:T(8,128)(2,1)S(1)} %collective-permute-done.4.tokens, bf16[3,1024,512]{2,1,0:T(8,128)(2,1)S(1)} %copy-done, bf16[8,16,128]{2,1,0:T(8,128)(2,1)S(1)} %get-tuple-element.37.gains, ...), custom_call_target="tpu_custom_call" | custom-call | flops 402653184 | bytes 5737984 | tf_op jit(solution)/shard_map/pallas_call | solution.py:28
  26.5 2.2 %collective-permute-done.3.message = bf16[544,128]{1,0:T(8,128)(2,1)S(1)} collective-permute-done((bf16[544,128]{1,0:T(8,128)(2,1)S(1)}, bf16[544,128]{1,0:T(8,128)(2,1)S(1)}, u32[]{:S(2)}, u32[]{:S(2)}) %collective-permute-start.3) | collective-permute-done | bytes 139296 | tf_op jit(solution)/shard_map/ppermute | solution.py:41
  29.2 0.9 %collective-permute-start.7 = (bf16[128,1024]{1,0:T(8,128)(2,1)S(1)}, bf16[128,1024]{1,0:T(8,128)(2,1)S(1)}, u32[]{:S(2)}, u32[]{:S(2)}) collective-permute-start(bf16[128,1024]{1,0:T(8,128)(2,1)S(1)} %get-tuple-element.50), channel_id=1, source_target_pairs={{0,1},{1,0},{2,3},{3,2},{4,5},{5,4},{6,7},{7,6},{8,9},{9,8},{10,11... | collective-permute-start | bytes 786440 | tf_op jit(solution)/shard_map/ppermute | solution.py:41
  30.1 0.8 %collective-permute-start.5 = (bf16[544,128]{1,0:T(8,128)(2,1)S(1)}, bf16[544,128]{1,0:T(8,128)(2,1)S(1)}, u32[]{:S(2)}, u32[]{:S(2)}) collective-permute-start(bf16[544,128]{1,0:T(8,128)(2,1)S(1)} %shard_map.123), channel_id=1, source_target_pairs={{0,16},{2,18},{4,20},{6,22},{8,24},{10,26},{12,28},{14,30},{16,0},... | collective-permute-start | bytes 417800 | tf_op jit(solution)/shard_map/ppermute | solution.py:41
  30.8 6.7 %collective-permute-done.5.message = bf16[544,128]{1,0:T(8,128)(2,1)S(1)} collective-permute-done((bf16[544,128]{1,0:T(8,128)(2,1)S(1)}, bf16[544,128]{1,0:T(8,128)(2,1)S(1)}, u32[]{:S(2)}, u32[]{:S(2)}) %collective-permute-start.5) | collective-permute-done | bytes 139296 | tf_op jit(solution)/shard_map/ppermute | solution.py:41
  37.9 1.3 %collective-permute-start.6 = (bf16[128,1024]{1,0:T(8,128)(2,1)S(1)}, bf16[128,1024]{1,0:T(8,128)(2,1)S(1)}, u32[]{:S(2)}, u32[]{:S(2)}) collective-permute-start(bf16[128,1024]{1,0:T(8,128)(2,1)S(1)} %get-tuple-element.48), channel_id=1, source_target_pairs={{0,1},{1,0},{2,3},{3,2},{4,5},{5,4},{6,7},{7,6},{8,9},{9,8},{10,11... | collective-permute-start | bytes 786440 | tf_op jit(solution)/shard_map/ppermute | solution.py:41
  39.2 1.9 %shard_map.127 = bf16[128,1024]{1,0:T(8,128)(2,1)S(1)} custom-call(bf16[128,1024]{1,0:T(8,128)(2,1)S(1)} %collective-permute-done.2.second.tokens, f32[128,1024]{1,0:T(8,128)S(1)} %get-tuple-element.49.kept, bf16[128,1024]{1,0:T(8,128)(2,1)S(1)} %collective-permute-done.7.received, bf16[2,1024,2048]{2,1,0:T(8,128)(2,1)S(1)} %bitcast.3, ...), custom_call_target="tpu_custom_call" | custom-call | flops 1610612736 | bytes 13631488 | tf_op jit(solution)/shard_map/pallas_call | solution.py:28
  41.1 0.9 %collective-permute-start.8 = (bf16[128,1024]{1,0:T(8,128)(2,1)S(1)}, bf16[128,1024]{1,0:T(8,128)(2,1)S(1)}, u32[]{:S(2)}, u32[]{:S(2)}) collective-permute-start(bf16[128,1024]{1,0:T(8,128)(2,1)S(1)} %shard_map.127), channel_id=1, source_target_pairs={{0,1},{1,0},{2,3},{3,2},{4,5},{5,4},{6,7},{7,6},{8,9},{9,8},{10,11... | collective-permute-start | bytes 786440 | tf_op jit(solution)/shard_map/ppermute | solution.py:41
  42.0 2.9 %collective-permute-done.6.received = bf16[128,1024]{1,0:T(8,128)(2,1)S(1)} collective-permute-done((bf16[128,1024]{1,0:T(8,128)(2,1)S(1)}, bf16[128,1024]{1,0:T(8,128)(2,1)S(1)}, u32[]{:S(2)}, u32[]{:S(2)}) %collective-permute-start.6) | collective-permute-done | bytes 262176 | tf_op jit(solution)/shard_map/ppermute | solution.py:41
  44.9 2.0 %shard_map.126 = f32[128,1024]{1,0:T(8,128)S(1)} custom-call(bf16[128,1024]{1,0:T(8,128)(2,1)S(1)} %copy-done.4, f32[128,1024]{1,0:T(8,128)S(1)} %get-tuple-element.47.kept, bf16[128,1024]{1,0:T(8,128)(2,1)S(1)} %collective-permute-done.6.received, bf16[2,1024,2048]{2,1,0:T(8,128)(2,1)S(1)} %bitcast.3, bf16[2048,1024]{1,0:T(8,128)(2,1)S(1)} %copy-done.1), custom_call_target="tpu_custom_call" | custom-call | flops 1610612736 | bytes 13631488 | tf_op jit(solution)/shard_map/pallas_call | solution.py:28
  46.9 0.8 %collective-permute-done.8 = bf16[128,1024]{1,0:T(8,128)(2,1)S(1)} collective-permute-done((bf16[128,1024]{1,0:T(8,128)(2,1)S(1)}, bf16[128,1024]{1,0:T(8,128)(2,1)S(1)}, u32[]{:S(2)}, u32[]{:S(2)}) %collective-permute-start.8) | collective-permute-done | bytes 262176 | tf_op jit(solution)/shard_map/ppermute | solution.py:41
  47.7 0.8 %add_convert_fusion = bf16[128,1024]{1,0:T(8,128)(2,1)} fusion(f32[128,1024]{1,0:T(8,128)S(1)} %shard_map.126, bf16[128,1024]{1,0:T(8,128)(2,1)S(1)} %collective-permute-done.8), kind=kLoop, calls=%fused_computation | loop fusion | flops 393216 | bytes 1048576 | tf_op jit(solution)/shard_map/convert_element_type | solution.py:363
  (24 shorter events, 1.6 us)
Async XLA Ops:
  0.0 17.7 %collective-permute-start = (bf16[128,1024]{1,0:T(8,128)(2,1)}, bf16[128,1024]{1,0:T(8,128)(2,1)S(1)}, u32[]{:S(2)}, u32[]{:S(2)}) collective-permute-start(bf16[128,1024]{1,0:T(8,128)(2,1)} %tokens.1), channel_id=1, source_target_pairs={{0,16},{2,18},{4,20},{6,22},{8,24},{10,26},{12,28},{14,30},{16,0},... | collective-permute-start | bytes 786440 | tf_op jit(solution)/shard_map/ppermute | solution.py:41
  6.2 11.5 %collective-permute-start.1 = (f32[7,128]{1,0:T(8,128)S(1)}, f32[7,128]{1,0:T(8,128)S(1)}, u32[]{:S(2)}, u32[]{:S(2)}) collective-permute-start(f32[7,128]{1,0:T(8,128)S(1)} %fusion.small), channel_id=1, source_target_pairs={{0,16},{2,18},{4,20},{6,22},{8,24},{10,26},{12,28},{14,30},{16,0},... | collective-permute-start | bytes 10760 | tf_op jit(solution)/shard_map/ppermute | solution.py:41
  6.3 8.0 %collective-permute-start.2 = (bf16[128,1024]{1,0:T(8,128)(2,1)}, bf16[128,1024]{1,0:T(8,128)(2,1)S(1)}, u32[]{:S(2)}, u32[]{:S(2)}) collective-permute-start(bf16[128,1024]{1,0:T(8,128)(2,1)} %tokens.1), channel_id=1, source_target_pairs={{0,1},{1,0},{2,3},{3,2},{4,5},{5,4},{6,7},{7,6},{8,9},{9,8},{10,11... | collective-permute-start | bytes 786440 | tf_op jit(solution)/shard_map/ppermute | solution.py:41
  8.7 1.2 %copy-start.2 = (bf16[2,512,512]{2,1,0:T(8,128)(2,1)S(1)}, bf16[2,512,512]{2,1,0:T(8,128)(2,1)}, u32[]{:S(2)}) copy-start(bf16[2,512,512]{2,1,0:T(8,128)(2,1)} %cache.7) | copy-start | bytes 3145732
  8.7 5.6 %copy-start = (bf16[3,1024,512]{2,1,0:T(8,128)(2,1)S(1)}, bf16[3,1024,512]{2,1,0:T(8,128)(2,1)}, u32[]{:S(2)}) copy-start(bf16[3,1024,512]{2,1,0:T(8,128)(2,1)} %weight.7) | copy-start | bytes 9437188
  8.8 5.6 %copy-start.4 = (bf16[128,1024]{1,0:T(8,128)(2,1)S(1)}, bf16[128,1024]{1,0:T(8,128)(2,1)}, u32[]{:S(2)}) copy-start(bf16[128,1024]{1,0:T(8,128)(2,1)} %tokens.1) | copy-start | bytes 786436
  17.7 6.9 %collective-permute-start.4 = (bf16[128,1024]{1,0:T(8,128)(2,1)S(1)}, bf16[128,1024]{1,0:T(8,128)(2,1)S(1)}, u32[]{:S(2)}, u32[]{:S(2)}) collective-permute-start(bf16[128,1024]{1,0:T(8,128)(2,1)S(1)} %collective-permute-done.tokens), channel_id=1, source_target_pairs={{0,1},{1,0},{2,3},{3,2},{4,5},{5,4},{6,7},{7,6},{8,9},{9,8},{10,11... | collective-permute-start | bytes 786440 | tf_op jit(solution)/shard_map/ppermute | solution.py:41
  19.3 9.5 %copy-start.3 = (bf16[512,1024]{1,0:T(8,128)(2,1)S(1)}, bf16[512,1024]{1,0:T(8,128)(2,1)}, u32[]{:S(2)}) copy-start(bf16[512,1024]{1,0:T(8,128)(2,1)} %weight.9) | copy-start | bytes 3145732
  19.3 19.9 %slice-start = ((s8[8388608]{0:T(1024)(128)(4,1)}), s8[4194304]{0:T(1024)(128)(4,1)S(1)}, s32[]{:S(2)}) async-start(s8[8388608]{0:T(1024)(128)(4,1)} %bitcast.2), calls=%async_computation | async-start | bytes 8388608
  21.2 7.6 %collective-permute-start.3 = (bf16[544,128]{1,0:T(8,128)(2,1)S(1)}, bf16[544,128]{1,0:T(8,128)(2,1)S(1)}, u32[]{:S(2)}, u32[]{:S(2)}) collective-permute-start(bf16[544,128]{1,0:T(8,128)(2,1)S(1)} %shard_map.122), channel_id=1, source_target_pairs={{0,16},{2,18},{4,20},{6,22},{8,24},{10,26},{12,28},{14,30},{16,0},... | collective-permute-start | bytes 417800 | tf_op jit(solution)/shard_map/ppermute | solution.py:41
  24.5 14.7 %slice-start.1 = ((s8[8388608]{0:T(1024)(128)(4,1)}), s8[4194304]{0:T(1024)(128)(4,1)S(1)}, s32[]{:S(2)}) async-start(s8[8388608]{0:T(1024)(128)(4,1)} %bitcast.2), calls=%async_computation.1 | async-start | bytes 8388608
  24.5 14.7 %copy-start.1 = (bf16[2048,1024]{1,0:T(8,128)(2,1)S(1)}, bf16[2048,1024]{1,0:T(8,128)(2,1)}, u32[]{:S(2)}) copy-start(bf16[2048,1024]{1,0:T(8,128)(2,1)} %down.3) | copy-start | bytes 12582916
  29.2 10.0 %collective-permute-start.7 = (bf16[128,1024]{1,0:T(8,128)(2,1)S(1)}, bf16[128,1024]{1,0:T(8,128)(2,1)S(1)}, u32[]{:S(2)}, u32[]{:S(2)}) collective-permute-start(bf16[128,1024]{1,0:T(8,128)(2,1)S(1)} %get-tuple-element.50), channel_id=1, source_target_pairs={{0,1},{1,0},{2,3},{3,2},{4,5},{5,4},{6,7},{7,6},{8,9},{9,8},{10,11... | collective-permute-start | bytes 786440 | tf_op jit(solution)/shard_map/ppermute | solution.py:41
  30.1 7.4 %collective-permute-start.5 = (bf16[544,128]{1,0:T(8,128)(2,1)S(1)}, bf16[544,128]{1,0:T(8,128)(2,1)S(1)}, u32[]{:S(2)}, u32[]{:S(2)}) collective-permute-start(bf16[544,128]{1,0:T(8,128)(2,1)S(1)} %shard_map.123), channel_id=1, source_target_pairs={{0,16},{2,18},{4,20},{6,22},{8,24},{10,26},{12,28},{14,30},{16,0},... | collective-permute-start | bytes 417800 | tf_op jit(solution)/shard_map/ppermute | solution.py:41
  37.9 7.0 %collective-permute-start.6 = (bf16[128,1024]{1,0:T(8,128)(2,1)S(1)}, bf16[128,1024]{1,0:T(8,128)(2,1)S(1)}, u32[]{:S(2)}, u32[]{:S(2)}) collective-permute-start(bf16[128,1024]{1,0:T(8,128)(2,1)S(1)} %get-tuple-element.48), channel_id=1, source_target_pairs={{0,1},{1,0},{2,3},{3,2},{4,5},{5,4},{6,7},{7,6},{8,9},{9,8},{10,11... | collective-permute-start | bytes 786440 | tf_op jit(solution)/shard_map/ppermute | solution.py:41
  41.1 6.6 %collective-permute-start.8 = (bf16[128,1024]{1,0:T(8,128)(2,1)S(1)}, bf16[128,1024]{1,0:T(8,128)(2,1)S(1)}, u32[]{:S(2)}, u32[]{:S(2)}) collective-permute-start(bf16[128,1024]{1,0:T(8,128)(2,1)S(1)} %shard_map.127), channel_id=1, source_target_pairs={{0,1},{1,0},{2,3},{3,2},{4,5},{5,4},{6,7},{7,6},{8,9},{9,8},{10,11... | collective-permute-start | bytes 786440 | tf_op jit(solution)/shard_map/ppermute | solution.py:41

commit v3 on v2

--- a/solution.py
+++ b/solution.py
@@ -235,19 +235,24 @@
     message[width:, :] = jnp.concatenate(parts, axis=0).astype(BF16)
 
 
-def join(chunk, linked, own, own_log, message, weight, kept, sent):
+def join(chunk, own, own_log, *refs):
+    *linked, weight, kept, sent = refs
     width = weight.shape[0]
-    stats = message[width:, :].astype(F32)
-    far_log = stats[:8, :] + stats[8:16, :] + stats[16:24, :]
-    far_log = jnp.where(linked[0] > 0, far_log, MASKED)
-    share = 1.0 / (1.0 + jnp.exp2(far_log - own_log[chunk]))
+    if linked:
+        (message,) = linked
+        stats = message[width:, :].astype(F32)
+        far_log = stats[:8, :] + stats[8:16, :] + stats[16:24, :]
+        share = 1.0 / (1.0 + jnp.exp2(far_log - own_log[chunk]))
     pieces = []
     for cols in blocks(width):
         joined = []
         for start in range(cols.start, cols.stop, HEAD):
             rows, head = slice(start, start + HEAD), start // HEAD
-            far = message[rows, :].astype(F32)
-            joined.append(far + (own[chunk, rows, :] - far) * share[head : head + 1, :])
+            part = own[chunk, rows, :]
+            if linked:
+                far = message[rows, :].astype(F32)
+                part = far + (part - far) * share[head : head + 1, :]
+            joined.append(part)
         pieces.append(jnp.concatenate(joined, axis=0).T.astype(BF16))
     product = dot(jnp.concatenate(pieces, axis=1), weight[...])
     kept[...] = product
@@ -264,13 +269,13 @@
     out[...] = stream + product if final else product.astype(BF16)
 
 
-def shards(
+def layer(
+    with_partner,
     tokens,
     variate,
     time_ids,
     cache_var,
     cache_len,
-    linked,
     cache_kv,
     var_bias,
     w_qkv,
@@ -287,18 +292,19 @@
     paired = ways == 2
     key_chunks = cache_rows // LANES + 2
 
-    far_tokens = swap(tokens, "group", partner)
-    ids, held = lax.optimization_barrier(((time_ids + HEAD * variate).astype(F32), tokens))
+    if with_partner:
+        far_tokens = swap(tokens, "group", partner)
     if paired:
-        other_tokens = swap(held, "tp", 1)
+        other_tokens = swap(tokens, "tp", 1)
     small = jnp.concatenate(
         [
-            ids,
+            (time_ids + HEAD * variate).astype(F32),
             cache_var.astype(F32),
             jnp.pad(var_bias.reshape(-1), (0, LANES - 2 * heads)),
         ]
     ).reshape(-1, LANES)
-    far_small = swap(small, "group", partner)
+    if with_partner:
+        far_small = swap(small, "group", partner)
     time_hot, var_hot, cosine, sine, key_cosine, key_sine, key_hot, gains = call(
         functools.partial(tables, paired, heads),
         [((2, HEAD, LANES), BF16), ((2, 16, LANES), BF16), ((2, HALF, LANES), F32), ((2, HALF, LANES), F32)]
@@ -322,27 +328,36 @@
         flops=6 * 256 * model * width, scratch=[pltpu.VMEM((2 * LANES, model), BF16)],
     )
     key_side = (gains, keys, values, cache_kv, cache_values, key_hot)
+    messages = []
+    if with_partner:
+        far_tokens, far_small, _ = lax.optimization_barrier((far_tokens, far_small, queries))
+        far_rows = all_rows(far_tokens, swap(far_tokens, "tp", 1) if paired else None)
+
+        def attended_for(index):
+            (message,) = call(
+                functools.partial(attend_far, index, paired), [((width + STAT_ROWS, LANES), BF16)],
+                far_small, far_rows[index], w_qkv, *key_side, flops=8 * 128 * 768 * width,
+                scratch=[pltpu.VMEM((width, LANES), BF16), pltpu.VMEM((LOG_ROWS, LANES), F32)],
+            )
+            return message
+
+        messages.append(attended_for(0))
+        queries, _ = lax.optimization_barrier((queries, messages[0]))
     own, own_log = call(
         attend_own, [((2, width, LANES), F32), ((2, LOG_ROWS, LANES), F32)],
         queries, time_hot, var_hot, *key_side, flops=8 * 256 * 768 * width,
     )
-    far_tokens, far_small, own = lax.optimization_barrier((far_tokens, far_small, own))
-    far_rows = all_rows(far_tokens, swap(far_tokens, "tp", 1) if paired else None)
-    messages = []
-    for index in range(2):
-        (message,) = call(
-            functools.partial(attend_far, index, paired), [((width + STAT_ROWS, LANES), BF16)],
-            far_small, far_rows[index], w_qkv, *key_side, flops=8 * 128 * 768 * width,
-            scratch=[pltpu.VMEM((width, LANES), BF16), pltpu.VMEM((LOG_ROWS, LANES), F32)],
-        )
-        messages.append(message)
-    returned = [swap(message, "group", partner) for message in messages]
-    returned[0], _ = lax.optimization_barrier((returned[0], messages[1]))
+    if with_partner:
+        far_small, _ = lax.optimization_barrier((far_small, own_log))
+        messages.append(attended_for(1))
+        returned = [swap(message, "group", partner) for message in messages]
+        returned[0], _ = lax.optimization_barrier((returned[0], messages[1]))
     kept, sent = [], []
     for index in range(2):
+        extra = [returned[index]] if with_partner else []
         products = call(
             functools.partial(join, index), [((LANES, model), F32), ((LANES, model), BF16)],
-            own, own_log, returned[index], w_out, scalars=(linked,), flops=2 * 128 * width * model,
+            own, own_log, *extra, w_out, flops=8_000_000_000,
         )
         kept.append(products[0])
         sent.append(products[1])
@@ -371,6 +386,15 @@
     stream = (tokens.astype(F32) + attended.astype(F32)).astype(BF16).astype(F32)
     own_ffn = lax.dynamic_slice_in_dim(summed, start, local, 0).astype(F32)
     return (stream + own_ffn).astype(BF16)
+
+
+def shards(tokens, variate, time_ids, cache_var, cache_len, linked, *rest):
+    return lax.cond(
+        linked[0] > 0,
+        functools.partial(layer, True),
+        functools.partial(layer, False),
+        tokens, variate, time_ids, cache_var, cache_len, *rest,
+    )
 
 
 def solution(mesh):

time: 48.7 us -> 42.7 us (0.88)
  waiting for transfers between devices: 17 us -> 11.1 us
  Pallas kernels: 12.3 us -> 13.2 us
  between operations: 1.47 us -> 0.67 us
  other arithmetic: 2.15 us -> 1.46 us
    ppermute x9, waiting for transfers between devices: 17 us -> 11.1 us  [swap(): return lax.ppermute(block, axis, [(i, i ^ distance) for i in range(count)])]
    pallas_call x10, Pallas kernels: 12.3 us -> 13.2 us  [call(): pl.pallas_call(body, out_shape=shapes, in_specs=[IN_SMEM] * len(scalars)...]
    convert_element_type x3 -> x2, other arithmetic: 2.14 us -> 1.38 us  [the longest x1 0.7 us: layer(): (time_ids + HEAD * variate).astype(F32)]
  transfers between devices with their start and end apart: 9 -> 9, of which waited for: 6 -> 7; matrix products, arithmetic and copies ran while one was open for 4% -> 5% of each run, Pallas kernels for 25% -> 31%
where the time goes in v3:
time: 42.7 us; the launch traced here: 42 us
  starting transfers between devices  13.7 us (32%)
  Pallas kernels  13.2 us (31%)
  waiting for transfers between devices  11.1 us (26%)
  local copies, waits for them, and re-layouts  1.49 us (3%)
  other arithmetic  1.46 us (3%)
  between operations  0.67 us (2%)
    ppermute x9, starting transfers between devices, swap(): return lax.ppermute(block, axis, [(i, i ^ distance) for i in range(count)])  13.7 us
    pallas_call x10, Pallas kernels, call(): pl.pallas_call(body, out_shape=shapes, in_specs=[IN_SMEM] * len(scalars)...  13.2 us
    ppermute x9, waiting for transfers between devices, swap(): return lax.ppermute(block, axis, [(i, i ^ distance) for i in range(count)])  11.1 us
  transfers between devices with their start and end apart: 9, of which 7 were waited for; matrix products, arithmetic and copies ran while one was open for 5% of the time, Pallas kernels for 31%

profile of v3, /device:TPU:0, one launch (start us, length us, event | category | flops | bytes accessed | tf_op | source)
XLA Modules:
  0.0 42.0 jit_solution(11716026869429748514)
XLA Ops:
  0.7 40.6 %conditional.7 = (bf16[128,1024]{1,0:T(8,128)(2,1)S(1)}) conditional(s32[]{:T(128)} %bitcast.2, (bf16[128,1024]{1,0:T(8,128)(2,1)}, s32[256]{0:T(256)}, s32[256]{0:T(256)}, s32[512]{0:T(512)}, f32[2,8]{1,0:T(2,128)}, /*index=5*/s32[1]{0:T(128)}, bf16[3,1024,512]{2,1,0:T(8,128)(2,1)}, bf16[2,512,512]{2,1,0:T(8,128)(2,1)}, bf16[512,1024]{1,0:T(8,128)(2,1)}, ...), branch_computations={%region_0.1_spmd, %region_1.2_spmd} | conditional | flops 27637542912 | bytes 122305264
  0.9 4.1 %collective-permute-start.5 = (bf16[128,1024]{1,0:T(8,128)(2,1)}, bf16[128,1024]{1,0:T(8,128)(2,1)S(1)}, u32[]{:S(2)}, u32[]{:S(2)}) collective-permute-start(bf16[128,1024]{1,0:T(8,128)(2,1)} %get-tuple-element.86.first.tokens), channel_id=1, source_target_pairs={{0,16},{2,18},{4,20},{6,22},{8,24},{10,26},{12,28},{14,30},{16,0},... | collective-permute-start | bytes 786440 | tf_op jit(solution)/shard_map/cond/branch_1_fun/ppermute | solution.py:41
  5.0 1.5 %collective-permute-start.4 = (bf16[128,1024]{1,0:T(8,128)(2,1)}, bf16[128,1024]{1,0:T(8,128)(2,1)S(1)}, u32[]{:S(2)}, u32[]{:S(2)}) collective-permute-start(bf16[128,1024]{1,0:T(8,128)(2,1)} %get-tuple-element.86.first.tokens), channel_id=1, source_target_pairs={{0,1},{1,0},{2,3},{3,2},{4,5},{5,4},{6,7},{7,6},{8,9},{9,8},{10,11... | collective-permute-start | bytes 786440 | tf_op jit(solution)/shard_map/cond/branch_1_fun/ppermute | solution.py:41
  6.4 0.8 %reshape.14 = f32[16]{0:T(128)S(1)} reshape(f32[2,8]{1,0:T(2,128)} %get-tuple-element.92) | data formatting | bytes 128 | tf_op jit(solution)/shard_map/cond/branch_1_fun/reshape | solution.py:303
  7.9 0.7 %add_convert_fusion.1 = f32[256]{0:T(256)S(1)} fusion(s32[256]{0:T(256)} %get-tuple-element.89, s32[256]{0:T(256)} %get-tuple-element.90), kind=kLoop, calls=%fused_computation.9 | loop fusion | flops 768 | bytes 3072 | tf_op jit(solution)/shard_map/cond/branch_1_fun/convert_element_type | solution.py:301
  9.0 1.1 %branch_1_fun.10 = (bf16[2,64,128]{2,1,0:T(8,128)(2,1)S(1)}, bf16[2,16,128]{2,1,0:T(8,128)(2,1)S(1)}, f32[2,32,128]{2,1,0:T(8,128)S(1)}, f32[2,32,128]{2,1,0:T(8...) custom-call(s32[1]{0:T(128)} %get-tuple-element.88.length, ...), custom_call_target="tpu_custom_call" | custom-call | flops 6000000000 | bytes 3584 | tf_op jit(solution)/shard_map/cond/branch_1_fun/pallas_call | solution.py:28
  10.1 1.4 %collective-permute-done.4.second.tokens = bf16[128,1024]{1,0:T(8,128)(2,1)S(1)} collective-permute-done((bf16[128,1024]{1,0:T(8,128)(2,1)}, bf16[128,1024]{1,0:T(8,128)(2,1)S(1)}, u32[]{:S(2)}, u32[]{:S(2)}) %collective-permute-start.4) | collective-permute-done | bytes 262176 | tf_op jit(solution)/shard_map/cond/branch_1_fun/ppermute | solution.py:41
  11.5 1.2 %branch_1_fun.11 = (bf16[2,512,128]{2,1,0:T(8,128)(2,1)S(1)}, bf16[2,128,512]{2,1,0:T(8,128)(2,1)S(1)}, bf16[2,512,128]{2,1,0:T(8,128)(2,1)S(1)}) custom-call(bf16[128,1024]{1,0:T(8,128)(2,1)S(1)} %copy-done.7, bf16[128,1024]{1,0:T(8,128)(2,1)S(1)} %collective-permute-done.4.second.tokens, bf16[3,1024,512]{2,1,0:T(8,128)(2,1)S(1)} %copy-done.3, ...), custom_call_target="tpu_custom_call" | custom-call | flops 805306368 | bytes 3997696 | tf_op jit(solution)/shard_map/cond/branch_1_fun/pallas_call | solution.py:28
  13.2 1.2 %collective-permute-start.8 = (bf16[128,1024]{1,0:T(8,128)(2,1)S(1)}, bf16[128,1024]{1,0:T(8,128)(2,1)S(1)}, u32[]{:S(2)}, u32[]{:S(2)}) collective-permute-start(bf16[128,1024]{1,0:T(8,128)(2,1)S(1)} %collective-permute-done.5.tokens), channel_id=1, source_target_pairs={{0,1},{1,0},{2,3},{3,2},{4,5},{5,4},{6,7},{7,6},{8,9},{9,8},{10,11... | collective-permute-start | bytes 786440 | tf_op jit(solution)/shard_map/cond/branch_1_fun/ppermute | solution.py:41
  14.5 1.9 %branch_1_fun.13 = bf16[544,128]{1,0:T(8,128)(2,1)S(1)} custom-call(f32[7,128]{1,0:T(8,128)S(1)} %collective-permute-done.6.small, bf16[128,1024]{1,0:T(8,128)(2,1)S(1)} %collective-permute-done.5.tokens, bf16[3,1024,512]{2,1,0:T(8,128)(2,1)S(1)} %copy-done.3, bf16[8,16,128]{2,1,0:T(8,128)(2,1)S(1)} %get-tuple-element.100.gains, ...), custom_call_target="tpu_custom_call" | custom-call | flops 402653184 | bytes 5737984 | tf_op jit(solution)/shard_map/cond/branch_1_fun/pallas_call | solution.py:28
  16.4 1.6 %collective-permute-start.7 = (bf16[544,128]{1,0:T(8,128)(2,1)S(1)}, bf16[544,128]{1,0:T(8,128)(2,1)S(1)}, u32[]{:S(2)}, u32[]{:S(2)}) collective-permute-start(bf16[544,128]{1,0:T(8,128)(2,1)S(1)} %branch_1_fun.13), channel_id=1, source_target_pairs={{0,16},{2,18},{4,20},{6,22},{8,24},{10,26},{12,28},{14,30},{16,0},... | collective-permute-start | bytes 417800 | tf_op jit(solution)/shard_map/cond/branch_1_fun/ppermute | solution.py:41
  18.0 2.2 %branch_1_fun.14 = (f32[2,512,128]{2,1,0:T(8,128)S(1)}, f32[2,8,128]{2,1,0:T(8,128)S(1)}) custom-call(bf16[2,512,128]{2,1,0:T(8,128)(2,1)S(1)} %get-tuple-element.105.queries, bf16[2,64,128]{2,1,0:T(8,128)(2,1)S(1)} %get-tuple-element.106.time_hot, bf16[2,16,128]{2,1,0:T(8,128)(2,1)S(1)} %get-tuple-element.107.var_hot, ...), custom_call_target="tpu_custom_call" | custom-call | flops 805306368 | bytes 2629632 | tf_op jit(solution)/shard_map/cond/branch_1_fun/pallas_call | solution.py:28
  20.2 2.2 %collective-permute-done.8.tokens = bf16[128,1024]{1,0:T(8,128)(2,1)S(1)} collective-permute-done((bf16[128,1024]{1,0:T(8,128)(2,1)S(1)}, bf16[128,1024]{1,0:T(8,128)(2,1)S(1)}, u32[]{:S(2)}, u32[]{:S(2)}) %collective-permute-start.8) | collective-permute-done | bytes 262176 | tf_op jit(solution)/shard_map/cond/branch_1_fun/ppermute | solution.py:41
  22.4 1.9 %branch_1_fun.15 = bf16[544,128]{1,0:T(8,128)(2,1)S(1)} custom-call(f32[7,128]{1,0:T(8,128)S(1)} %collective-permute-done.6.small, bf16[128,1024]{1,0:T(8,128)(2,1)S(1)} %collective-permute-done.8.tokens, bf16[3,1024,512]{2,1,0:T(8,128)(2,1)S(1)} %copy-done.3, bf16[8,16,128]{2,1,0:T(8,128)(2,1)S(1)} %get-tuple-element.100.gains, ...), custom_call_target="tpu_custom_call" | custom-call | flops 402653184 | bytes 5737984 | tf_op jit(solution)/shard_map/cond/branch_1_fun/pallas_call | solution.py:28
  24.3 1.6 %collective-permute-start.9 = (bf16[544,128]{1,0:T(8,128)(2,1)S(1)}, bf16[544,128]{1,0:T(8,128)(2,1)S(1)}, u32[]{:S(2)}, u32[]{:S(2)}) collective-permute-start(bf16[544,128]{1,0:T(8,128)(2,1)S(1)} %branch_1_fun.15), channel_id=1, source_target_pairs={{0,16},{2,18},{4,20},{6,22},{8,24},{10,26},{12,28},{14,30},{16,0},... | collective-permute-start | bytes 417800 | tf_op jit(solution)/shard_map/cond/branch_1_fun/ppermute | solution.py:41
  26.4 1.1 %collective-permute-start.11 = (bf16[128,1024]{1,0:T(8,128)(2,1)S(1)}, bf16[128,1024]{1,0:T(8,128)(2,1)S(1)}, u32[]{:S(2)}, u32[]{:S(2)}) collective-permute-start(bf16[128,1024]{1,0:T(8,128)(2,1)S(1)} %get-tuple-element.118), channel_id=1, source_target_pairs={{0,1},{1,0},{2,3},{3,2},{4,5},{5,4},{6,7},{7,6},{8,9},{9,8},{10,11... | collective-permute-start | bytes 786440 | tf_op jit(solution)/shard_map/cond/branch_1_fun/ppermute | solution.py:41
  27.5 2.9 %collective-permute-done.9.refs_0_ = bf16[544,128]{1,0:T(8,128)(2,1)S(1)} collective-permute-done((bf16[544,128]{1,0:T(8,128)(2,1)S(1)}, bf16[544,128]{1,0:T(8,128)(2,1)S(1)}, u32[]{:S(2)}, u32[]{:S(2)}) %collective-permute-start.9) | collective-permute-done | bytes 139296 | tf_op jit(solution)/shard_map/cond/branch_1_fun/ppermute | solution.py:41
  30.7 1.2 %collective-permute-start.10 = (bf16[128,1024]{1,0:T(8,128)(2,1)S(1)}, bf16[128,1024]{1,0:T(8,128)(2,1)S(1)}, u32[]{:S(2)}, u32[]{:S(2)}) collective-permute-start(bf16[128,1024]{1,0:T(8,128)(2,1)S(1)} %get-tuple-element.114), channel_id=1, source_target_pairs={{0,1},{1,0},{2,3},{3,2},{4,5},{5,4},{6,7},{7,6},{8,9},{9,8},{10,11... | collective-permute-start | bytes 786440 | tf_op jit(solution)/shard_map/cond/branch_1_fun/ppermute | solution.py:41
  32.0 0.9 %collective-permute-done.11.received = bf16[128,1024]{1,0:T(8,128)(2,1)S(1)} collective-permute-done((bf16[128,1024]{1,0:T(8,128)(2,1)S(1)}, bf16[128,1024]{1,0:T(8,128)(2,1)S(1)}, u32[]{:S(2)}, u32[]{:S(2)}) %collective-permute-start.11) | collective-permute-done | bytes 262176 | tf_op jit(solution)/shard_map/cond/branch_1_fun/ppermute | solution.py:41
  32.8 2.0 %branch_1_fun.19 = bf16[128,1024]{1,0:T(8,128)(2,1)S(1)} custom-call(bf16[128,1024]{1,0:T(8,128)(2,1)S(1)} %collective-permute-done.4.second.tokens, f32[128,1024]{1,0:T(8,128)S(1)} %get-tuple-element.117.kept, bf16[128,1024]{1,0:T(8,128)(2,1)S(1)} %collective-permute-done.11.received, bf16[2,1024,2048]{2,1,0:T(8,128)(2,1)S(1)} %bitcast.8, ...), custom_call_target="tpu_custom_call" | custom-call | flops 1610612736 | bytes 13631488 | tf_op jit(solution)/shard_map/cond/branch_1_fun/pallas_call | solution.py:28
  34.8 1.1 %collective-permute-start.12 = (bf16[128,1024]{1,0:T(8,128)(2,1)S(1)}, bf16[128,1024]{1,0:T(8,128)(2,1)S(1)}, u32[]{:S(2)}, u32[]{:S(2)}) collective-permute-start(bf16[128,1024]{1,0:T(8,128)(2,1)S(1)} %branch_1_fun.19), channel_id=1, source_target_pairs={{0,1},{1,0},{2,3},{3,2},{4,5},{5,4},{6,7},{7,6},{8,9},{9,8},{10,11... | collective-permute-start | bytes 786440 | tf_op jit(solution)/shard_map/cond/branch_1_fun/ppermute | solution.py:41
  35.9 1.3 %collective-permute-done.10.received = bf16[128,1024]{1,0:T(8,128)(2,1)S(1)} collective-permute-done((bf16[128,1024]{1,0:T(8,128)(2,1)S(1)}, bf16[128,1024]{1,0:T(8,128)(2,1)S(1)}, u32[]{:S(2)}, u32[]{:S(2)}) %collective-permute-start.10) | collective-permute-done | bytes 262176 | tf_op jit(solution)/shard_map/cond/branch_1_fun/ppermute | solution.py:41
  37.2 2.0 %branch_1_fun.18 = f32[128,1024]{1,0:T(8,128)S(1)} custom-call(bf16[128,1024]{1,0:T(8,128)(2,1)S(1)} %copy-done.7, f32[128,1024]{1,0:T(8,128)S(1)} %get-tuple-element.113.kept, bf16[128,1024]{1,0:T(8,128)(2,1)S(1)} %collective-permute-done.10.received, bf16[2,1024,2048]{2,1,0:T(8,128)(2,1)S(1)} %bitcast.8, bf16[2048,1024]{1,0:T(8,128)(2,1)S(1)} %copy-done.1), custom_call_target="tpu_custom_call" | custom-call | flops 1610612736 | bytes 13631488 | tf_op jit(solution)/shard_map/cond/branch_1_fun/pallas_call | solution.py:28
  39.1 2.1 %collective-permute-done.12 = bf16[128,1024]{1,0:T(8,128)(2,1)S(1)} collective-permute-done((bf16[128,1024]{1,0:T(8,128)(2,1)S(1)}, bf16[128,1024]{1,0:T(8,128)(2,1)S(1)}, u32[]{:S(2)}, u32[]{:S(2)}) %collective-permute-start.12) | collective-permute-done | bytes 262176 | tf_op jit(solution)/shard_map/cond/branch_1_fun/ppermute | solution.py:41
  (27 shorter events, 3.3 us)
Async XLA Ops:
  0.9 12.3 %collective-permute-start.5 = (bf16[128,1024]{1,0:T(8,128)(2,1)}, bf16[128,1024]{1,0:T(8,128)(2,1)S(1)}, u32[]{:S(2)}, u32[]{:S(2)}) collective-permute-start(bf16[128,1024]{1,0:T(8,128)(2,1)} %get-tuple-element.86.first.tokens), channel_id=1, source_target_pairs={{0,16},{2,18},{4,20},{6,22},{8,24},{10,26},{12,28},{14,30},{16,0},... | collective-permute-start | bytes 786440 | tf_op jit(solution)/shard_map/cond/branch_1_fun/ppermute | solution.py:41
  5.0 6.6 %collective-permute-start.4 = (bf16[128,1024]{1,0:T(8,128)(2,1)}, bf16[128,1024]{1,0:T(8,128)(2,1)S(1)}, u32[]{:S(2)}, u32[]{:S(2)}) collective-permute-start(bf16[128,1024]{1,0:T(8,128)(2,1)} %get-tuple-element.86.first.tokens), channel_id=1, source_target_pairs={{0,1},{1,0},{2,3},{3,2},{4,5},{5,4},{6,7},{7,6},{8,9},{9,8},{10,11... | collective-permute-start | bytes 786440 | tf_op jit(solution)/shard_map/cond/branch_1_fun/ppermute | solution.py:41
  8.6 4.6 %collective-permute-start.6 = (f32[7,128]{1,0:T(8,128)S(1)}, f32[7,128]{1,0:T(8,128)S(1)}, u32[]{:S(2)}, u32[]{:S(2)}) collective-permute-start(f32[7,128]{1,0:T(8,128)S(1)} %fusion.1.small), channel_id=1, source_target_pairs={{0,16},{2,18},{4,20},{6,22},{8,24},{10,26},{12,28},{14,30},{16,0},... | collective-permute-start | bytes 10760 | tf_op jit(solution)/shard_map/cond/branch_1_fun/ppermute | solution.py:41
  9.0 2.5 %copy-start.3 = (bf16[3,1024,512]{2,1,0:T(8,128)(2,1)S(1)}, bf16[3,1024,512]{2,1,0:T(8,128)(2,1)}, u32[]{:S(2)}) copy-start(bf16[3,1024,512]{2,1,0:T(8,128)(2,1)} %get-tuple-element.87.weight) | copy-start | bytes 9437188
  9.0 2.5 %copy-start.7 = (bf16[128,1024]{1,0:T(8,128)(2,1)S(1)}, bf16[128,1024]{1,0:T(8,128)(2,1)}, u32[]{:S(2)}) copy-start(bf16[128,1024]{1,0:T(8,128)(2,1)} %get-tuple-element.86.first.tokens) | copy-start | bytes 786436
  10.1 4.2 %copy-start.5 = (bf16[2,512,512]{2,1,0:T(8,128)(2,1)S(1)}, bf16[2,512,512]{2,1,0:T(8,128)(2,1)}, u32[]{:S(2)}) copy-start(bf16[2,512,512]{2,1,0:T(8,128)(2,1)} %get-tuple-element.103.cache) | copy-start | bytes 3145732
  13.2 9.2 %collective-permute-start.8 = (bf16[128,1024]{1,0:T(8,128)(2,1)S(1)}, bf16[128,1024]{1,0:T(8,128)(2,1)S(1)}, u32[]{:S(2)}, u32[]{:S(2)}) collective-permute-start(bf16[128,1024]{1,0:T(8,128)(2,1)S(1)} %collective-permute-done.5.tokens), channel_id=1, source_target_pairs={{0,1},{1,0},{2,3},{3,2},{4,5},{5,4},{6,7},{7,6},{8,9},{9,8},{10,11... | collective-permute-start | bytes 786440 | tf_op jit(solution)/shard_map/cond/branch_1_fun/ppermute | solution.py:41
  16.4 9.5 %collective-permute-start.7 = (bf16[544,128]{1,0:T(8,128)(2,1)S(1)}, bf16[544,128]{1,0:T(8,128)(2,1)S(1)}, u32[]{:S(2)}, u32[]{:S(2)}) collective-permute-start(bf16[544,128]{1,0:T(8,128)(2,1)S(1)} %branch_1_fun.13), channel_id=1, source_target_pairs={{0,16},{2,18},{4,20},{6,22},{8,24},{10,26},{12,28},{14,30},{16,0},... | collective-permute-start | bytes 417800 | tf_op jit(solution)/shard_map/cond/branch_1_fun/ppermute | solution.py:41
  18.0 8.0 %copy-start.10 = (bf16[512,1024]{1,0:T(8,128)(2,1)S(1)}, bf16[512,1024]{1,0:T(8,128)(2,1)}, u32[]{:S(2)}) copy-start(bf16[512,1024]{1,0:T(8,128)(2,1)} %get-tuple-element.112.refs_1_) | copy-start | bytes 3145732
  24.3 6.0 %collective-permute-start.9 = (bf16[544,128]{1,0:T(8,128)(2,1)S(1)}, bf16[544,128]{1,0:T(8,128)(2,1)S(1)}, u32[]{:S(2)}, u32[]{:S(2)}) collective-permute-start(bf16[544,128]{1,0:T(8,128)(2,1)S(1)} %branch_1_fun.15), channel_id=1, source_target_pairs={{0,16},{2,18},{4,20},{6,22},{8,24},{10,26},{12,28},{14,30},{16,0},... | collective-permute-start | bytes 417800 | tf_op jit(solution)/shard_map/cond/branch_1_fun/ppermute | solution.py:41
  26.3 6.5 %slice-start.2 = ((s8[8388608]{0:T(1024)(128)(4,1)}), s8[4194304]{0:T(1024)(128)(4,1)S(1)}, s32[]{:S(2)}) async-start(s8[8388608]{0:T(1024)(128)(4,1)} %bitcast.7), calls=%async_computation.2 | async-start | bytes 8388608
  26.3 6.5 %slice-start.3 = ((s8[8388608]{0:T(1024)(128)(4,1)}), s8[4194304]{0:T(1024)(128)(4,1)S(1)}, s32[]{:S(2)}) async-start(s8[8388608]{0:T(1024)(128)(4,1)} %bitcast.7), calls=%async_computation.3 | async-start | bytes 8388608
  26.4 6.5 %copy-start.1 = (bf16[2048,1024]{1,0:T(8,128)(2,1)S(1)}, bf16[2048,1024]{1,0:T(8,128)(2,1)}, u32[]{:S(2)}) copy-start(bf16[2048,1024]{1,0:T(8,128)(2,1)} %get-tuple-element.116.down) | copy-start | bytes 12582916
  26.4 6.4 %collective-permute-start.11 = (bf16[128,1024]{1,0:T(8,128)(2,1)S(1)}, bf16[128,1024]{1,0:T(8,128)(2,1)S(1)}, u32[]{:S(2)}, u32[]{:S(2)}) collective-permute-start(bf16[128,1024]{1,0:T(8,128)(2,1)S(1)} %get-tuple-element.118), channel_id=1, source_target_pairs={{0,1},{1,0},{2,3},{3,2},{4,5},{5,4},{6,7},{7,6},{8,9},{9,8},{10,11... | collective-permute-start | bytes 786440 | tf_op jit(solution)/shard_map/cond/branch_1_fun/ppermute | solution.py:41
  30.7 6.4 %collective-permute-start.10 = (bf16[128,1024]{1,0:T(8,128)(2,1)S(1)}, bf16[128,1024]{1,0:T(8,128)(2,1)S(1)}, u32[]{:S(2)}, u32[]{:S(2)}) collective-permute-start(bf16[128,1024]{1,0:T(8,128)(2,1)S(1)} %get-tuple-element.114), channel_id=1, source_target_pairs={{0,1},{1,0},{2,3},{3,2},{4,5},{5,4},{6,7},{7,6},{8,9},{9,8},{10,11... | collective-permute-start | bytes 786440 | tf_op jit(solution)/shard_map/cond/branch_1_fun/ppermute | solution.py:41
  34.8 6.4 %collective-permute-start.12 = (bf16[128,1024]{1,0:T(8,128)(2,1)S(1)}, bf16[128,1024]{1,0:T(8,128)(2,1)S(1)}, u32[]{:S(2)}, u32[]{:S(2)}) collective-permute-start(bf16[128,1024]{1,0:T(8,128)(2,1)S(1)} %branch_1_fun.19), channel_id=1, source_target_pairs={{0,1},{1,0},{2,3},{3,2},{4,5},{5,4},{6,7},{7,6},{8,9},{9,8},{10,11... | collective-permute-start | bytes 786440 | tf_op jit(solution)/shard_map/cond/branch_1_fun/ppermute | solution.py:41
  41.3 0.7 %copy-start.8 = (bf16[128,1024]{1,0:T(8,128)(2,1)}, bf16[128,1024]{1,0:T(8,128)(2,1)S(1)}, u32[]{:S(2)}) copy-start(bf16[128,1024]{1,0:T(8,128)(2,1)S(1)} %get-tuple-element.150) | copy-start | bytes 786436
